TPU v7x, 128 devices: a whole 4x4x4 slice. The times are simulated.
128 devices in a mesh: gx: 16 (over x, z), gy: 8 (over y, core).
Axes of the slice: x: 4, y: 4, z: 4, core: 2. Of those that a mesh axis runs over, the one named last changes fastest.
Arguments:
- features: bfloat16 [16, 8, 16, 8, 8, 768], P('gx', 'gy'), may hold values from -12 to 12
- voxel_mask: int32 [16, 8, 16, 512], P('gx', 'gy'), may hold values 0 or 1
- occupancy: int32 [32, 16, 8], P('gx', 'gy'), may hold values from -1 to 15, as said below
- send_counts: int32 [8, 16, 16], P('gy'), may hold values from 0 to 1, as said below
- weight_one: bfloat16 [27, 96, 128], replicated, may hold values from -0.125 to 0.125
- bias_one: float32 [128], replicated, may hold values from -3 to 3
- weight_two: bfloat16 [27, 128, 128], replicated, may hold values from -0.109375 to 0.109375
- bias_two: float32 [128], replicated, may hold values from -3 to 3
- cotangent: bfloat16 [16, 8, 8, 8, 8, 1024], P('gx', 'gy'), may hold values from -12 to 12
Outputs:
- result: bfloat16 [16, 8, 8, 8, 8, 1024], P('gx', 'gy')
- grad_one: float32 [27, 96, 128], replicated
- grad_two: float32 [27, 128, 128], replicated
Inputs may be any that keep to these rules, and one draw needn't show every extreme that they name: `occupancy`: A device's active bricks fill its slots 0 to n - 1 with n at most 16; in every row of tiles along gx the active bricks average 8 per device, and some device holds exactly 16. Row d of send_counts[r] sums to that device's active bricks; every column sums to exactly 8.
All inputs are finite; a program needn't handle non-finite values. No bound on the sum of `voxel_mask` on one device may be relied on, other than what follows from the above.
Results may differ from a plain program's by a relative error of at most 0.0067.
Values may be sent and summed in bfloat16 or wider, within the bound.
A program may use at most 192 MiB of HBM per device.

v0:
```python
import jax
import jax.numpy as jnp
from jax import lax
from jax.sharding import PartitionSpec as P


def padded_2(cells, sides, width):
    for axis, dim in sides:
        count = lax.axis_size(axis)
        ends = count - 1
        head = lax.slice_in_dim(cells, 0, width, axis=dim)
        tail = lax.slice_in_dim(cells, cells.shape[dim] - width, cells.shape[dim], axis=dim)
        cells = jnp.concatenate(
            [
                lax.ppermute(tail, axis, [(i, (i + 1) % count) for i in range(ends)]),
                cells,
                lax.ppermute(head, axis, [((i + 1) % count, i) for i in range(ends)]),
            ],
            axis=dim,
        )
    return cells


def for_sending(value):
    return jax.tree.map(lambda a: a.astype(jnp.bfloat16) if a.dtype == jnp.float32 else a, value)


def silu_slope(value):
    sig = jax.nn.sigmoid(value)
    return sig * (1.0 + value * (1.0 - sig))


def conv_bricks(padded, kernel, layout):
    return lax.conv_general_dilated(
        padded,
        kernel,
        (1, 1, 1),
        "VALID",
        dimension_numbers=("NDHWC", layout, "NDHWC"),
        preferred_element_type=jnp.float32,
    )


def tap_products(padded, slopes):
    return lax.conv_general_dilated(
        padded,
        slopes,
        (1, 1, 1),
        "VALID",
        dimension_numbers=("CDHWN", "IDHWO", "DHWNC"),
        preferred_element_type=jnp.float32,
    )


def keep_rows(flags, rows):
    shaped = flags.reshape(flags.shape + (1,) * (rows.ndim - 1))
    return jnp.where(shaped, rows, jnp.zeros((), rows.dtype))


def place_rows(rows, flags, index):
    safe = jnp.clip(index, 0, rows.shape[0] - 1)
    return keep_rows(flags, rows[safe])


def pick_rows(rows, flags, order, count):
    lanes = jnp.arange(flags.shape[0], dtype=jnp.int32)
    wanted = jnp.arange(count, dtype=jnp.int32)[:, None]
    hits = flags[None, :] & (order[None, :] == wanted)
    index = jnp.sum(jnp.where(hits, lanes[None, :], 0), axis=1)
    return keep_rows(jnp.any(hits, axis=1), rows[index])


def slot_places(occupancy, slots):
    tiles_x, tiles_y, tiles_z = occupancy.shape
    flat = occupancy.reshape(-1)
    spots = jnp.arange(flat.shape[0], dtype=jnp.int32)
    match = flat[None, :] == jnp.arange(slots, dtype=jnp.int32)[:, None]
    found = jnp.sum(jnp.where(match, spots[None, :], 0), axis=1)
    live = jnp.any(match, axis=1)
    col_z = found % tiles_z
    col_y = found // tiles_z % tiles_y
    col_x = found // (tiles_z * tiles_y)
    return (col_x, col_y, col_z, live)


def route_plan(send_counts, capacity):
    own_index = lax.axis_index("gx")
    table = send_counts[0]
    outgoing = table[own_index]
    incoming = table[:, own_index]
    start = jnp.cumsum(outgoing) - outgoing
    lanes = jnp.arange(capacity, dtype=jnp.int32)
    out_slot = (start[:, None] + lanes[None, :]).reshape(-1)
    out_live = (lanes[None, :] < outgoing[:, None]).reshape(-1)
    in_live = (lanes[None, :] < incoming[:, None]).reshape(-1)
    rank = jnp.cumsum(in_live.astype(jnp.int32)) - 1
    return (out_slot, out_live, in_live, rank)


def densify(bricks, occupancy, channels):
    slots = bricks.shape[0]
    tiles_x, tiles_y, tiles_z = occupancy.shape
    table = jnp.concatenate([bricks, jnp.zeros((1,) + bricks.shape[1:], bricks.dtype)], 0)
    index = jnp.where(occupancy < 0, slots, occupancy)
    placed = table[index].reshape(tiles_x, tiles_y, tiles_z, 8, 8, 8, channels)
    placed = placed.transpose(0, 3, 1, 4, 2, 5, 6)
    return placed.reshape(tiles_x * 8, tiles_y * 8, tiles_z * 8 * channels)


def extend(volume, along_x, along_y):
    faces = jnp.stack([volume[0], volume[-1]])
    wide = along_x(faces)
    volume = jnp.concatenate([wide[0:1], volume, wide[3:4]], axis=0)
    faces = jnp.stack([volume[:, 0], volume[:, -1]])
    wide = along_y(faces)
    return jnp.concatenate([wide[0][:, None], volume, wide[3][:, None]], axis=1)


def padded_bricks(extended, places, channels):
    rows_x, rows_y, merged = extended.shape
    grid = extended.reshape(rows_x, rows_y, merged // channels, channels)
    grid = jnp.pad(grid, ((0, 0), (0, 0), (1, 1), (0, 0)))
    col_x, col_y, col_z = places
    zero = jnp.zeros((), jnp.int32)

    def padded_cut(spot_x, spot_y, spot_z):
        return lax.dynamic_slice(
            grid, (spot_x * 8, spot_y * 8, spot_z * 8, zero), (10, 10, 10, channels)
        )

    return jax.vmap(padded_cut)(col_x, col_y, col_z)


def first_layer(pads, mask, weight_one, bias_one):
    c_in = weight_one.shape[1]
    c_mid = weight_one.shape[2]
    count = pads.shape[0]
    kernel = weight_one.reshape(3, 3, 3, c_in, c_mid)
    linear = conv_bricks(pads, kernel, "DHWIO") + bias_one
    active = mask.reshape(count, 8, 8, 8, 1).astype(jnp.float32)
    hidden_rows = (
        (active * jax.nn.silu(linear)).astype(jnp.bfloat16).reshape(count, 8, 8, 8 * c_mid)
    )
    gate_rows = (active * silu_slope(linear)).astype(jnp.bfloat16).reshape(count, 8, 8, 8 * c_mid)
    return (hidden_rows, gate_rows)


def second_layer(pads, mask, slopes, weight_two, bias_two):
    c_mid = weight_two.shape[1]
    c_out = weight_two.shape[2]
    count = pads.shape[0]
    kernel = weight_two.reshape(3, 3, 3, c_mid, c_out)
    linear = conv_bricks(pads, kernel, "DHWIO") + bias_two
    active = mask.reshape(count, 8, 8, 8, 1).astype(jnp.float32)
    output = (active * jax.nn.silu(linear)).astype(jnp.bfloat16)
    slope_live = (
        slopes.reshape(count, 8, 8, 8, c_out).astype(jnp.float32) * active * silu_slope(linear)
    ).astype(jnp.bfloat16)
    total = tap_products(pads, slope_live).reshape(27 * c_mid, c_out)
    return (
        total,
        output.reshape(count, 8, 8, 8 * c_out),
        slope_live.reshape(count, 8, 8, 8 * c_out),
    )


def spread_back(slopes, weight_two):
    c_mid = weight_two.shape[1]
    c_out = weight_two.shape[2]
    count = slopes.shape[0]
    flipped = weight_two.reshape(3, 3, 3, c_mid, c_out)[::-1, ::-1, ::-1]
    wide = jnp.pad(slopes.reshape(count, 8, 8, 8, c_out), ((0, 0), (2, 2), (2, 2), (2, 2), (0, 0)))
    spread = conv_bricks(wide, flipped, "DHWOI")
    return spread.astype(jnp.bfloat16)


def first_weights(pads, slopes, c_in, c_mid):
    count = pads.shape[0]
    total = tap_products(pads, slopes.reshape(count, 8, 8, 8, c_mid))
    return total.reshape(27 * c_in, c_mid)


def gradient_home(spread_home, places, tiles, channels):
    tiles_x, tiles_y, tiles_z = tiles
    col_x, col_y, col_z = places
    zero = jnp.zeros((), jnp.int32)
    canvas = jnp.zeros((8 * tiles_x + 2, 8 * tiles_y + 2, 8 * tiles_z + 2, channels), jnp.float32)

    def deposit(index, canvas):
        piece = spread_home[index].reshape(10, 10, 10, channels).astype(jnp.float32)
        corner = (col_x[index] * 8, col_y[index] * 8, col_z[index] * 8, zero)
        current = lax.dynamic_slice(canvas, corner, (10, 10, 10, channels))
        return lax.dynamic_update_slice(canvas, current + piece, corner)

    canvas = lax.fori_loop(0, spread_home.shape[0], deposit, canvas)
    merged = canvas[:, :, 1:-1].reshape(8 * tiles_x + 2, 8 * tiles_y + 2, 8 * tiles_z * channels)
    edges = jnp.stack([merged[:, 0], merged[:, -1]])
    wide = padded_2(edges.astype(jnp.bfloat16), (("gy", 0),), 1).astype(edges.dtype)
    merged = merged[:, 1:-1]
    merged = merged.at[:, 0].add(wide[0]).at[:, -1].add(wide[3])
    edges = jnp.stack([merged[0], merged[-1]])
    wide = padded_2(edges.astype(jnp.bfloat16), (("gx", 0),), 1).astype(edges.dtype)
    merged = merged[1:-1]
    merged = merged.at[0].add(wide[0]).at[-1].add(wide[3])
    grid = merged.reshape(8 * tiles_x, 8 * tiles_y, 8 * tiles_z, channels)

    def gradient_cut(spot_x, spot_y, spot_z):
        return lax.dynamic_slice(
            grid, (spot_x * 8, spot_y * 8, spot_z * 8, zero), (8, 8, 8, channels)
        )

    return jax.vmap(gradient_cut)(col_x, col_y, col_z)


def normalized(grad):
    return grad * lax.rsqrt(jnp.mean(grad * grad) + 1e-05)


def body(
    features,
    voxel_mask,
    occupancy,
    send_counts,
    weight_one,
    bias_one,
    weight_two,
    bias_two,
    cotangent,
):
    peers = lax.axis_size("gx")
    slots = features.shape[2]
    work = cotangent.shape[2]
    capacity = (slots + peers - 1) // peers
    c_in = weight_one.shape[1]
    c_mid = weight_one.shape[2]
    c_out = weight_two.shape[2]
    col_x, col_y, col_z, live = slot_places(occupancy, slots)
    places = (col_x, col_y, col_z)
    mask_home = keep_rows(live, voxel_mask[0, 0]).astype(jnp.bfloat16)
    inputs = features[0, 0].reshape(slots, 8, 8, 8, c_in) * mask_home.reshape(slots, 8, 8, 8, 1)
    inputs = inputs.reshape(slots, 8, 8, 8 * c_in)
    out_slot, out_live, in_live, rank = route_plan(send_counts, capacity)
    volume = densify(inputs, occupancy, c_in)
    extended = extend(
        volume,
        lambda faces: padded_2(faces, (("gx", 0),), 1),
        lambda faces: padded_2(faces, (("gy", 0),), 1),
    )
    pads = padded_bricks(extended, places, c_in)
    sent = place_rows(pads, out_live, out_slot)
    sent_mask = place_rows(mask_home, out_live, out_slot)
    arrived, arrived_mask = (
        lax.all_to_all(sent, "gx", split_axis=0, concat_axis=0, tiled=True),
        lax.all_to_all(sent_mask, "gx", split_axis=0, concat_axis=0, tiled=True),
    )
    work_pads = pick_rows(arrived, in_live, rank, work)
    work_mask = pick_rows(arrived_mask, in_live, rank, work)
    hidden_work, gate_work = first_layer(work_pads, work_mask, weight_one, bias_one)
    returned, returned_gate = (
        lax.all_to_all(
            place_rows(hidden_work, in_live, rank), "gx", split_axis=0, concat_axis=0, tiled=True
        ),
        lax.all_to_all(
            place_rows(gate_work, in_live, rank), "gx", split_axis=0, concat_axis=0, tiled=True
        ),
    )
    hidden = pick_rows(returned, out_live, out_slot, slots)
    gate_home = pick_rows(returned_gate, out_live, out_slot, slots)
    volume_two = densify(hidden, occupancy, c_mid)
    extended_two = extend(
        volume_two,
        lambda faces: padded_2(faces, (("gx", 0),), 1),
        lambda faces: padded_2(faces, (("gy", 0),), 1),
    )
    pads_two = padded_bricks(extended_two, places, c_mid)
    arrived_two = lax.all_to_all(
        place_rows(pads_two, out_live, out_slot), "gx", split_axis=0, concat_axis=0, tiled=True
    )
    work_pads_two = pick_rows(arrived_two, in_live, rank, work)
    grad_two, result, slopes = second_layer(
        work_pads_two, work_mask, cotangent[0, 0], weight_two, bias_two
    )
    spread_work = spread_back(slopes, weight_two)
    returned_two = lax.all_to_all(
        for_sending(place_rows(spread_work, in_live, rank)),
        "gx",
        split_axis=0,
        concat_axis=0,
        tiled=True,
    )
    spread_home = pick_rows(returned_two, out_live, out_slot, slots)
    back_one = gradient_home(spread_home, places, occupancy.shape, c_mid)
    gate_float = gate_home.reshape(slots, 8, 8, 8, c_mid).astype(jnp.float32)
    slope_home = (back_one * gate_float).astype(jnp.bfloat16).reshape(slots, 8, 8, 8 * c_mid)
    arrived_slopes = lax.all_to_all(
        place_rows(slope_home, out_live, out_slot), "gx", split_axis=0, concat_axis=0, tiled=True
    )
    slope_work = pick_rows(arrived_slopes, in_live, rank, work)
    grad_one = first_weights(work_pads, slope_work, c_in, c_mid)
    grad_one, grad_two = lax.psum((grad_one, grad_two), ("gx", "gy"))
    return (
        result[None, None],
        normalized(grad_one).reshape(27, c_in, c_mid),
        normalized(grad_two).reshape(27, c_mid, c_out),
    )


def solution(mesh):
    placed = (
        P("gx", "gy", None, None, None, None),
        P("gx", "gy", None, None),
        P("gx", "gy", None),
        P("gy", None, None),
        P(),
        P(),
        P(),
        P(),
        P("gx", "gy", None, None, None, None),
    )
    return jax.shard_map(
        body,
        mesh=mesh,
        in_specs=placed,
        out_specs=(P("gx", "gy", None, None, None, None), P(), P()),
        check_vma=False,
    )
```

profile of v0, /device:TPU:1, one launch (start us, length us, event | category | flops | bytes accessed | tf_op | source)
XLA Modules:
  0.0 1382.2 jit_solution(110461578015506557)
XLA Ops:
  13.1 8.4 all-to-all-start
  32.3 8.2 reshape.639
  45.9 8.6 reshape.640
  82.1 8.4 select_maximum_fusion.2
  90.4 74.3 %while.25 = (s32[]{:T(128)}, bf16[18,18,66,96]{3,2,1,0:T(8,128)(2,1)}, s32[16,4]{0,1:T(4,128)S(1)}, bf16[16,10,10,10,96]{4,3,2,1,0:T(8,128)(2,1)}) while((s32[]{:T(128)}, bf16[18,18,66,96]{3,2,1,0:T(8,128)(2,1)}, s32[16,4]{0,1:T(4,128)S(1)}, bf16[16,10,10,10,96]{4,3,2,1,0:T(8,128)(2,1)}) %tuple.142), condition=%wide.while_cond.4.clone, body=%wide.while_body.4.sunk.clone | while | flops 2 | bytes 820861 | solution.py:127
  164.7 6.9 gather_fusion.3
  171.6 6.0 broadcast_select_fusion.2
  177.6 14.6 %reshape.884 = bf16[16,2,48000]{2,1,0:T(2,128)(2,1)} reshape(bf16[16,10,10,10,96]{4,3,2,1,0:T(8,128)(2,1)} %broadcast_select_fusion.2) | data formatting | bytes 6144000
  192.2 9.9 all-to-all-start.1
  203.6 40.7 %all-to-all-done.1 = bf16[16,2,48000]{2,1,0:T(2,128)(2,1)} async-done(((bf16[16,2,48000]{2,1,0:T(2,128)(2,1)}), bf16[16,2,48000]{2,1,0:T(2,128)(2,1)}, u32[]{:S(2)}, u32[]{:S(2)}) %all-to-all-start.1) | async-done | bytes 3072032 | tf_op jit(solution)/shard_map/all_to_all | solution.py:253
  244.3 14.7 %reshape.885 = bf16[16,10,10,10,96]{4,3,2,1,0:T(8,128)(2,1)} reshape(bf16[16,2,48000]{2,1,0:T(2,128)(2,1)} %all-to-all-done.1) | data formatting | bytes 6144000
  266.8 8.8 multiply_convert_fusion.1
  289.1 9.9 all-to-all-start.2
  299.5 28.7 %all-to-all-done.2 = bf16[16,8,8,1024]{3,2,1,0:T(8,128)(2,1)S(1)} async-done(((bf16[16,8,8,1024]{3,2,1,0:T(8,128)(2,1)}), bf16[16,8,8,1024]{3,2,1,0:T(8,128)(2,1)S(1)}, u32[]{:S(2)}, u32[]{:S(2)}) %all-to-all-start.2) | async-done | bytes 2097184 | tf_op jit(solution)/shard_map/all_to_all | solution.py:260
  346.4 7.4 collective-permute-done.5
  355.0 5.7 collective-permute-start.7
  372.5 8.5 select_maximum_fusion
  380.9 73.6 %while.26 = (s32[]{:T(128)}, bf16[18,18,66,128]{3,2,1,0:T(8,128)(2,1)}, s32[16,4]{0,1:T(4,128)S(1)}, bf16[16,10,10,10,128]{4,3,2,1,0:T(8,128)(2,1)}) while((s32[]{:T(128)}, bf16[18,18,66,128]{3,2,1,0:T(8,128)(2,1)}, s32[16,4]{0,1:T(4,128)S(1)}, bf16[16,10,10,10,128]{4,3,2,1,0:T(8,128)(2,1)}) %tuple.158), condition=%wide.while_cond.5.clone, body=%wide.while_body.5.sunk.clone | while | flops 2 | bytes 820861 | solution.py:127
  454.5 6.9 gather_fusion.8
  461.4 6.0 broadcast_select_fusion.3
  467.5 7.4 all-to-all-start.3
  476.5 84.0 %all-to-all-done.3 = bf16[16,10,10,10,128]{4,3,2,1,0:T(8,128)(2,1)} async-done(((bf16[16,10,10,10,128]{4,3,2,1,0:T(8,128)(2,1)}), bf16[16,10,10,10,128]{4,3,2,1,0:T(8,128)(2,1)}, u32[]{:S(2)}, u32[]{:S(2)}) %all-to-all-start.3) | async-done | bytes 4096032 | tf_op jit(solution)/shard_map/all_to_all | solution.py:276
  568.7 10.6 fusion.14
  579.3 14.8 %convolution_convert_fusion = bf16[8,10,10,10,128]{4,0,3,2,1:T(8,128)(2,1)S(1)} fusion(bf16[8,8,8,8,128]{4,0,3,2,1:T(8,128)(2,1)S(1)} %get-tuple-element.306, bf16[3,3,3,128,128]{4,3,2,1,0:T(8,128)(2,1)S(1)} %bitcast.203), kind=kOutput, calls=%fused_computation.65 | convolution fusion | flops 3624902656 | bytes 3981312 | tf_op jit(solution)/shard_map/conv_general_dilated | solution.py:34
  596.4 6.1 gather_fusion.10
  602.5 6.1 broadcast_select_fusion
  608.6 29.9 %all-to-all-start.4 = ((bf16[16,10,10,10,128]{4,3,2,1,0:T(8,128)(2,1)}), bf16[16,10,10,10,128]{4,3,2,1,0:T(8,128)(2,1)}, u32[]{:S(2)}, u32[]{:S(2)}) async-start(bf16[16,10,10,10,128]{4,3,2,1,0:T(8,128)(2,1)} %broadcast_select_fusion), calls=%async_computation.4 | async-start | bytes 13107200 | tf_op jit(solution)/shard_map/all_to_all | solution.py:284
  638.5 101.7 %all-to-all-done.4 = bf16[16,10,10,10,128]{4,3,2,1,0:T(8,128)(2,1)} async-done(((bf16[16,10,10,10,128]{4,3,2,1,0:T(8,128)(2,1)}), bf16[16,10,10,10,128]{4,3,2,1,0:T(8,128)(2,1)}, u32[]{:S(2)}, u32[]{:S(2)}) %all-to-all-start.4) | async-done | bytes 4096032 | tf_op jit(solution)/shard_map/all_to_all | solution.py:284
  740.3 7.0 gather_fusion.11
  747.3 6.1 broadcast_select_fusion.1
  758.6 176.4 %while.24 = (s32[]{:T(128)}, f32[18,18,66,128]{3,2,1,0:T(8,128)}, s32[16]{0:T(128)S(1)}, s32[16]{0:T(128)S(1)}, s32[16]{0:T(128)S(1)}, /*index=5*/bf16[16,10,10,10,128]{4,3,2,1,0:T(8,128)(2,1)}, s32[1]{0:T(128)}) while((s32[]{:T(128)}, f32[18,18,66,128]{3,2,1,0:T(8,128)}, s32[16]{0:T(128)S(1)}, s32[16]{0:T(128)S(1)}, ...), condition=%wide.region_9.10_spmd.clone, body=%wide.region_8.9_spmd.sunk.clone | while | flops 256014 | bytes 2304279 | solution.py:195
  763.8 5.8 dynamic_update_slice.9
  774.8 5.7 dynamic_update_slice.9
  785.8 5.8 dynamic_update_slice.9
  796.8 5.8 dynamic_update_slice.9
  807.8 5.8 dynamic_update_slice.9
  818.8 5.8 dynamic_update_slice.9
  829.9 5.8 dynamic_update_slice.9
  840.9 5.8 dynamic_update_slice.9
  851.9 5.8 dynamic_update_slice.9
  863.0 5.8 dynamic_update_slice.9
  874.0 5.8 dynamic_update_slice.9
  885.0 5.8 dynamic_update_slice.9
  896.1 5.8 dynamic_update_slice.9
  907.1 5.8 dynamic_update_slice.9
  918.1 5.8 dynamic_update_slice.9
  929.1 5.8 dynamic_update_slice.9
  934.9 10.1 slice.163
  945.0 10.2 copy.219
  955.3 12.3 reshape.646
  967.6 9.0 convert.17
  983.6 9.1 all-to-all-start.5
  992.6 10.5 slice.271
  1007.5 8.1 convert.18
  1028.7 9.2 slice.276
  1042.6 10.8 scatter-add.16
  1057.9 10.7 scatter-add.19
  1068.6 8.2 copy.254
  1076.8 70.3 %while.27 = (s32[]{:T(128)}, f32[16,16,64,128]{3,2,0,1:T(8,128)}, s32[16,4]{0,1:T(4,128)S(1)}, f32[16,8,8,8,128]{4,3,2,1,0:T(8,128)}) while((s32[]{:T(128)}, f32[16,16,64,128]{3,2,0,1:T(8,128)}, s32[16,4]{0,1:T(4,128)S(1)}, f32[16,8,8,8,128]{4,3,2,1,0:T(8,128)}) %tuple.159), condition=%wide.while_cond.6.clone, body=%wide.while_body.6.sunk.clone | while | flops 2 | bytes 525949 | solution.py:208
  1163.9 7.4 all-to-all-start.6
  1171.6 14.5 %fusion.15 = f32[3,3,3,128,128]{4,3,2,1,0:T(8,128)} fusion(bf16[8,8,8,8,128]{4,0,3,2,1:T(8,128)(2,1)S(1)} %get-tuple-element.306, bf16[8,10,10,10,128]{4,3,2,1,0:T(8,128)(2,1)} %copy-done.5), kind=kOutput, calls=%fused_computation.69 | convolution fusion | flops 3623878656 | bytes 4866048 | tf_op jit(solution)/shard_map/conv_general_dilated | solution.py:45
  1186.1 10.9 all-to-all-done.6
  1201.2 11.3 fusion.19
  1215.3 150.9 %all-reduce.7.cloned.1.call-done = (f32[2592,128]{1,0:T(8,128)}, f32[3456,128]{1,0:T(8,128)}) async-done(((f32[2592,128]{1,0:T(8,128)}, f32[3456,128]{1,0:T(8,128)}), (f32[2592,128]{1,0:T(8,128)}, f32[3456,128]{1,0:T(8,128)})) %all-reduce.7.cloned.1.call-update) | async-done | bytes 3096592 | tf_op jit(solution)/shard_map/psum | solution.py:300
  (391 shorter events, 456.2 us)
Async XLA Ops:
  7.2 561.3 %copy-start = (bf16[27,128,128]{2,1,0:T(8,128)(2,1)S(1)}, bf16[27,128,128]{2,1,0:T(8,128)(2,1)}, u32[]{:S(2)}) copy-start(bf16[27,128,128]{2,1,0:T(8,128)(2,1)} %param.25) | copy-start | bytes 2654212
  13.1 179.1 %all-to-all-start = ((bf16[16,2,256]{2,1,0:T(2,128)(2,1)}), bf16[16,2,256]{2,1,0:T(2,128)(2,1)S(1)}, u32[]{:S(2)}, u32[]{:S(2)}) async-start(bf16[16,2,256]{2,1,0:T(2,128)(2,1)} %reshape.886), calls=%async_computation | async-start | bytes 32768 | tf_op jit(solution)/shard_map/all_to_all | solution.py:254
  56.9 11.6 collective-permute-start.1
  58.2 11.1 collective-permute-start
  70.6 10.8 collective-permute-start.3
  74.7 7.0 collective-permute-start.2
  192.2 9.9 copy-start.12
  192.2 52.1 %all-to-all-start.1 = ((bf16[16,2,48000]{2,1,0:T(2,128)(2,1)}), bf16[16,2,48000]{2,1,0:T(2,128)(2,1)}, u32[]{:S(2)}, u32[]{:S(2)}) async-start(bf16[16,2,48000]{2,1,0:T(2,128)(2,1)} %reshape.884), calls=%async_computation.1 | async-start | bytes 6144000 | tf_op jit(solution)/shard_map/all_to_all | solution.py:253
  202.6 357.9 %copy-start.13 = (s32[1024]{0:T(1024)}, s32[1024]{0:T(1024)S(1)}, u32[]{:S(2)}) copy-start(s32[1024]{0:T(1024)S(1)} %pad_clamp_fusion.3) | copy-start | bytes 12292
  202.7 363.3 %copy-start.14 = (pred[8]{0:T(512)(128)(4,1)}, pred[8]{0:T(512)(128)(4,1)S(1)}, u32[]{:S(2)}) copy-start(pred[8]{0:T(512)(128)(4,1)S(1)} %fusion.46) | copy-start | bytes 28
  203.6 63.2 %copy-start.9 = (f32[8,8,8,8]{0,3,2,1:T(8,128)}, f32[8,8,8,8]{0,3,2,1:T(8,128)S(1)}, u32[]{:S(2)}) copy-start(f32[8,8,8,8]{0,3,2,1:T(8,128)S(1)} %select_convert_fusion.1) | copy-start | bytes 49156
  264.5 2.3 copy-start.16
  264.5 2.3 copy-start.17
  266.8 8.9 copy-start.3
  289.1 39.0 %all-to-all-start.2 = ((bf16[16,8,8,1024]{3,2,1,0:T(8,128)(2,1)}), bf16[16,8,8,1024]{3,2,1,0:T(8,128)(2,1)S(1)}, u32[]{:S(2)}, u32[]{:S(2)}) async-start(bf16[16,8,8,1024]{3,2,1,0:T(8,128)(2,1)} %get-tuple-element.315), calls=%async_computation.2 | async-start | bytes 4194304 | tf_op jit(solution)/shard_map/all_to_all | solution.py:260
  341.1 12.7 collective-permute-start.5
  342.4 12.3 collective-permute-start.4
  355.0 16.2 %collective-permute-start.7 = (bf16[1,18,8192]{2,1,0:T(8,128)(2,1)S(1)}, bf16[1,18,8192]{2,1,0:T(8,128)(2,1)}, u32[]{:S(2)}, u32[]{:S(2)}) collective-permute-start(bf16[1,18,8192]{2,1,0:T(8,128)(2,1)S(1)} %get-tuple-element.297), channel_id=1, source_target_pairs={{1,0},{2,1},{3,2},{4,3},{5,4},{6,5},{7,6},{9,8},{10,9},{11,10},{12... | collective-permute-start | bytes 884744 | tf_op jit(solution)/shard_map/ppermute | solution.py:17
  360.7 11.6 collective-permute-start.6
  467.5 7.4 copy-start.7
  467.5 93.1 %all-to-all-start.3 = ((bf16[16,10,10,10,128]{4,3,2,1,0:T(8,128)(2,1)}), bf16[16,10,10,10,128]{4,3,2,1,0:T(8,128)(2,1)}, u32[]{:S(2)}, u32[]{:S(2)}) async-start(bf16[16,10,10,10,128]{4,3,2,1,0:T(8,128)(2,1)} %broadcast_select_fusion.3), calls=%async_computation.3 | async-start | bytes 13107200 | tf_op jit(solution)/shard_map/all_to_all | solution.py:276
  566.1 2.6 copy-start.6
  566.1 2.6 copy-start.10
  566.1 2.6 copy-start.18
  568.5 10.8 copy-start.5
  608.6 131.6 %all-to-all-start.4 = ((bf16[16,10,10,10,128]{4,3,2,1,0:T(8,128)(2,1)}), bf16[16,10,10,10,128]{4,3,2,1,0:T(8,128)(2,1)}, u32[]{:S(2)}, u32[]{:S(2)}) async-start(bf16[16,10,10,10,128]{4,3,2,1,0:T(8,128)(2,1)} %broadcast_select_fusion), calls=%async_computation.4 | async-start | bytes 13107200 | tf_op jit(solution)/shard_map/all_to_all | solution.py:284
  977.7 25.5 %collective-permute-start.9 = (bf16[1,18,8192]{2,1,0:T(8,128)(2,1)S(1)}, bf16[1,18,8192]{2,1,0:T(8,128)(2,1)S(1)}, u32[]{:S(2)}, u32[]{:S(2)}) collective-permute-start(bf16[1,18,8192]{2,1,0:T(8,128)(2,1)S(1)} %get-tuple-element.293), channel_id=1, source_target_pairs={{1,0},{2,1},{3,2},{4,3},{5,4},{6,5},{7,6},{9,8},{10,9},{11,10},{12... | collective-permute-start | bytes 884744 | tf_op jit(solution)/shard_map/ppermute | solution.py:17
  981.6 21.5 %collective-permute-start.8 = (bf16[1,18,8192]{2,1,0:T(8,128)(2,1)S(1)}, bf16[1,18,8192]{2,1,0:T(8,128)(2,1)S(1)}, u32[]{:S(2)}, u32[]{:S(2)}) collective-permute-start(bf16[1,18,8192]{2,1,0:T(8,128)(2,1)S(1)} %get-tuple-element.292), channel_id=1, source_target_pairs={{0,1},{1,2},{2,3},{3,4},{4,5},{5,6},{6,7},{8,9},{9,10},{10,11},{11... | collective-permute-start | bytes 884744 | tf_op jit(solution)/shard_map/ppermute | solution.py:15
  983.6 41.5 %all-to-all-start.5 = ((bf16[16,8,8,1024]{3,2,1,0:T(8,128)(2,1)}), bf16[16,8,8,1024]{3,2,1,0:T(8,128)(2,1)}, u32[]{:S(2)}, u32[]{:S(2)}) async-start(bf16[16,8,8,1024]{3,2,1,0:T(8,128)(2,1)} %get-tuple-element.314), calls=%async_computation.5 | async-start | bytes 4194304 | tf_op jit(solution)/shard_map/all_to_all | solution.py:263
  1019.0 19.0 %collective-permute-start.11 = (bf16[1,16,8192]{2,0,1:T(2,128)(2,1)S(1)}, bf16[1,16,8192]{2,0,1:T(2,128)(2,1)S(1)}, u32[]{:S(2)}, u32[]{:S(2)}) collective-permute-start(bf16[1,16,8192]{2,0,1:T(2,128)(2,1)S(1)} %get-tuple-element.295), channel_id=1, source_target_pairs={{8,0},{16,8},{24,16},{32,24},{40,32},{48,40},{56,48},{64,56},{72,6... | collective-permute-start | bytes 786440 | tf_op jit(solution)/shard_map/ppermute | solution.py:17
  1020.3 17.7 %collective-permute-start.10 = (bf16[1,16,8192]{2,0,1:T(2,128)(2,1)S(1)}, bf16[1,16,8192]{2,0,1:T(2,128)(2,1)}, u32[]{:S(2)}, u32[]{:S(2)}) collective-permute-start(bf16[1,16,8192]{2,0,1:T(2,128)(2,1)S(1)} %get-tuple-element.294), channel_id=1, source_target_pairs={{0,8},{8,16},{16,24},{24,32},{32,40},{40,48},{48,56},{56,64},{64,7... | collective-permute-start | bytes 786440 | tf_op jit(solution)/shard_map/ppermute | solution.py:15
  1068.6 8.2 copy-start.11
  1163.9 33.1 %all-to-all-start.6 = ((bf16[16,8,8,1024]{3,2,1,0:T(8,128)(2,1)}), bf16[16,8,8,1024]{3,2,1,0:T(8,128)(2,1)}, u32[]{:S(2)}, u32[]{:S(2)}) async-start(bf16[16,8,8,1024]{3,2,1,0:T(8,128)(2,1)} %broadcast_select_fusion.6), calls=%async_computation.6 | async-start | bytes 4194304 | tf_op jit(solution)/shard_map/all_to_all | solution.py:295
  1171.3 194.8 %all-reduce.7.cloned.1.call-start = ((), (), s32[]{:S(2)}) async-start(), calls=%async_computation.7 | async-start | bytes 6193152 | tf_op jit(solution)/shard_map/psum | solution.py:300
  1186.1 13.5 copy-start.15
  1199.3 1.9 copy-start.4
  1212.5 1.2 copy-start.8
  1366.2 5.7 copy-start.2
  1369.3 5.6 copy-start.1
Sparse Core Ops, SparseCore 0:
  1212.7 153.4 all-reduce.6
where the time goes:
time: 1400 us; the launch traced here: 1380 us
  local copies, waits for them, and re-layouts  591 us (42%)
  waiting for transfers between devices  426 us (30%)
  other arithmetic  136 us (10%)
  starting transfers between devices  120 us (9%)
  matrix products  60 us (4%)
  loops' own time  31.7 us (2%)
  between operations  16.6 us (1%)
    gather x144, local copies, waits for them, and re-layouts  218 us
    psum x1, waiting for transfers between devices, body(): grad_one, grad_two = lax.psum((grad_one, grad_two), ('gx', 'gy'))  151 us
    all_to_all x1, waiting for transfers between devices, body(): lax.all_to_all(for_sending(place_rows(spread_work, in_live, rank)), 'gx',...  102 us
    dynamic_update_slice x16, local copies, waits for them, and re-layouts, deposit(): return lax.dynamic_update_slice(canvas, current + piece, corner)  92.5 us
    all_to_all x1, waiting for transfers between devices, body(): lax.all_to_all(place_rows(pads_two, out_live, out_slot), 'gx', split_axis...  84 us
    unnamed x51, local copies, waits for them, and re-layouts  45.1 us
    all_to_all x1, waiting for transfers between devices, body(): lax.all_to_all(sent, 'gx', split_axis=0, concat_axis=0, tiled=True)  40.7 us
    select_n x12, other arithmetic, keep_rows(): return jnp.where(shaped, rows, jnp.zeros((), rows.dtype))  39.4 us
  transfers between devices with their start and end apart: 20, of which 10 were waited for; matrix products, arithmetic and copies ran while one was open for 16% of the time, Pallas kernels for 0%

commit v1 on v0

v1 whole, which is shorter than its diff:
```python
import functools

import jax
import jax.numpy as jnp
from jax import lax
from jax.experimental import pallas as pl
from jax.experimental.pallas import tpu as pltpu
from jax.sharding import PartitionSpec as P

MESH = pl.DeviceIdType.MESH
F32 = jnp.float32
BF16 = jnp.bfloat16
C = 128
BRICK = 8 * C
LINE = 8 * BRICK
WIDE = LINE + 2 * C
PATCH = BRICK + 2 * C
LIMIT = 60 * 1024 * 1024

VMEM = pl.BlockSpec(memory_space=pltpu.VMEM)
SMEM = pl.BlockSpec(memory_space=pltpu.SMEM)
ANY = pl.BlockSpec(memory_space=pl.ANY)

VOLUME = jax.ShapeDtypeStruct((16, 2, 8, LINE), BF16)
FACES = jax.ShapeDtypeStruct((2, 2, 8, LINE), BF16)
CORNERS = jax.ShapeDtypeStruct((4, 8, BRICK), BF16)


def coords(place):
    return place // 16, lax.rem(place // 8, 2), lax.rem(place, 8)


def put(vol, faces, spot, lane, value):
    xb, yb, zb = spot
    lanes = pl.ds(pl.multiple_of(zb * BRICK + lane, C), value.shape[2])
    vol[pl.ds(xb * 8, 8), yb, :, lanes] = value.astype(BF16)
    row = jnp.where(yb == 0, value[:, 0, :], value[:, 7, :])
    faces[yb, xb, :, lanes] = row.astype(BF16)


def put_corners(faces, corners):
    for side_y in range(2):
        for side_x in range(2):
            face = faces[side_y, side_x].astype(F32)
            row = face[7 * side_x : 7 * side_x + 1]
            rows = [row[:, z * BRICK : (z + 1) * BRICK] for z in range(8)]
            corners[2 * side_y + side_x] = jnp.concatenate(rows, axis=0).astype(BF16)


def volume_kernel(info, feat, mask, vol, faces, corners):
    vol[...] = jnp.zeros(vol.shape, BF16)
    faces[...] = jnp.zeros(faces.shape, BF16)
    c_in = feat.shape[3] // 8

    def step(place, _):
        slot = info[place]

        @pl.when(slot >= 0)
        def _():
            rows = feat[slot].astype(F32)
            keep = mask[slot].reshape(8, 8, 8)
            pieces = []
            for w in range(8):
                pieces.append(rows[:, :, w * c_in : (w + 1) * c_in] * keep[:, :, w : w + 1])
                pieces.append(jnp.zeros((8, 8, C - c_in), F32))
            put(vol, faces, coords(place), 0, jnp.concatenate(pieces, axis=2))

        return 0

    lax.fori_loop(0, 32, step, 0)
    put_corners(faces, corners)


def halo_kernel(vol, faces, corners, x_halo, y_halo, c_halo, send_sem, recv_sem):
    nx, ny = lax.axis_size("gx"), lax.axis_size("gy")
    x, y = lax.axis_index("gx"), lax.axis_index("gy")
    left, right = lax.rem(x + nx - 1, nx), lax.rem(x + 1, nx)
    down, up = lax.rem(y + ny - 1, ny), lax.rem(y + 1, ny)
    plan = [
        (vol.at[0], x_halo.at[1], (left, y)),
        (vol.at[15], x_halo.at[0], (right, y)),
        (faces.at[0], y_halo.at[1], (x, down)),
        (faces.at[1], y_halo.at[0], (x, up)),
        (corners.at[0], c_halo.at[3], (left, down)),
        (corners.at[1], c_halo.at[2], (right, down)),
        (corners.at[2], c_halo.at[1], (left, up)),
        (corners.at[3], c_halo.at[0], (right, up)),
    ]
    barrier = pltpu.get_barrier_semaphore()
    for _, _, device in plan:
        pl.semaphore_signal(barrier, inc=1, device_id=device, device_id_type=MESH)
    pl.semaphore_wait(barrier, len(plan))
    copies = []
    for number, (source, target, device) in enumerate(plan):
        copy = pltpu.make_async_remote_copy(
            src_ref=source,
            dst_ref=target,
            send_sem=send_sem.at[number],
            recv_sem=recv_sem.at[number],
            device_id=device,
            device_id_type=MESH,
        )
        copy.start()
        copies.append(copy)
    for copy in copies:
        copy.wait()


def halo_exchange(vol, faces, corners, number):
    return pl.pallas_call(
        halo_kernel,
        out_shape=(jax.ShapeDtypeStruct((2, 2, 8, LINE), BF16), FACES, CORNERS),
        in_specs=[ANY] * 3,
        out_specs=(ANY,) * 3,
        scratch_shapes=[pltpu.SemaphoreType.DMA((8,)), pltpu.SemaphoreType.DMA((8,))],
        compiler_params=pltpu.CompilerParams(collective_id=number, has_side_effects=True),
        name="halo",
    )(vol, faces, corners)


def load_volume(info, own, x_halo, y_halo, c_halo, wide, sems):
    inner = pl.ds(C, LINE)
    copies = [
        pltpu.make_async_copy(own, wide.at[pl.ds(1, 16), pl.ds(1, 2), :, inner], sems.at[0]),
        pltpu.make_async_copy(x_halo.at[0], wide.at[0, pl.ds(1, 2), :, inner], sems.at[1]),
        pltpu.make_async_copy(x_halo.at[1], wide.at[17, pl.ds(1, 2), :, inner], sems.at[2]),
    ]
    for copy in copies:
        copy.start()
    margin = jnp.zeros((18, 4, 8, C), BF16)
    wide[:, :, :, 0:C] = margin
    wide[:, :, :, C + LINE : WIDE] = margin
    for side in range(2):
        block = 3 * side
        inside_y = info[34 + side] > 0
        for half in range(2):
            face = jnp.where(inside_y, y_halo[side, half].astype(F32), 0.0)
            for row in range(8):
                wide[1 + 8 * half + row, block, :, inner] = jnp.broadcast_to(
                    face[row : row + 1], (8, LINE)
                ).astype(BF16)
        for end in range(2):
            inside = inside_y & (info[32 + end] > 0)
            corner = jnp.where(inside, c_halo[2 * side + end].astype(F32), 0.0)
            for z in range(8):
                wide[17 * end, block, :, pl.ds(C + z * BRICK, BRICK)] = jnp.broadcast_to(
                    corner[z : z + 1], (8, BRICK)
                ).astype(BF16)
    for copy in copies:
        copy.wait()
    for end in range(2):

        @pl.when(info[32 + end] == 0)
        def _():
            wide[17 * end, 1:3, :, inner] = jnp.zeros((2, 8, LINE), BF16)


def cut_patch(wide, spot, even, odd):
    xb, yb, zb = spot
    lanes = pl.ds(pl.multiple_of(zb * BRICK, C), PATCH)
    rows = pl.ds(xb * 8, 10)
    before = wide[rows, yb, :, lanes].astype(F32)
    here = wide[rows, yb + 1, :, lanes].astype(F32)
    after = wide[rows, yb + 2, :, lanes].astype(F32)
    line = lax.broadcasted_iota(jnp.int32, here.shape, 1)
    shifts = [
        pltpu.roll(jnp.where(line == 7, before, here), 1, 1),
        here,
        pltpu.roll(jnp.where(line == 0, after, here), 7, 1),
    ]
    for b in range(3):
        even[b] = shifts[b].reshape(80, PATCH).astype(BF16)
        odd[b] = shifts[b][1:9].reshape(64, PATCH).astype(BF16)


def window(even, odd, a, b):
    parts = []
    for j in range(4):
        lanes = pl.ds(2 * C * j, 4 * C)
        parts.append(odd[b, :, lanes] if a == 1 else even[b, pl.ds(8 * a, 64), lanes])
    return jnp.concatenate(parts, axis=0)


def fill_band(band, taps):
    depth = taps.shape[1]
    band[...] = jnp.zeros(band.shape, BF16)
    for tap in range(9):
        for c in range(3):
            for o in range(2):
                band[tap, pl.ds((c + o) * C, depth), pl.ds(o * C, C)] = taps[3 * tap + c]


def convolve(even, odd, band):
    total = jnp.zeros((256, 2 * C), F32)
    for a in range(3):
        for b in range(3):
            total = total + jnp.dot(
                window(even, odd, a, b), band[3 * a + b], preferred_element_type=F32
            )
    return total


def add_taps(sums, slopes, even, odd):
    turned = slopes.T.astype(BF16)
    for a in range(3):
        for b in range(3):
            sums[3 * a + b] += jnp.dot(
                turned, window(even, odd, a, b), preferred_element_type=F32
            )


def gather_taps(sums, grad):
    depth = grad.shape[1]
    for tap in range(9):
        for c in range(3):
            part = (
                sums[tap, 0:C, c * C : (c + 1) * C]
                + sums[tap, C : 2 * C, (c + 1) * C : (c + 2) * C]
            )
            grad[3 * tap + c] = part.T[0:depth]


def spread_mask(keep):
    blocks = []
    for j in range(4):
        pair = [jnp.broadcast_to(keep[:, 2 * j + o : 2 * j + o + 1], (64, C)) for o in range(2)]
        blocks.append(jnp.concatenate(pair, axis=1))
    return jnp.concatenate(blocks, axis=0)


def sigmoid(value):
    return 1.0 / (1.0 + jnp.exp(-value))


def first_kernel(
    info, own, x_halo, y_halo, c_halo, mask, taps, bias,
    vol, faces, corners, gates,
    wide, band, even, odd, sems,
):
    load_volume(info, own, x_halo, y_halo, c_halo, wide, sems)
    fill_band(band, taps)
    vol[...] = jnp.zeros(vol.shape, BF16)
    faces[...] = jnp.zeros(faces.shape, BF16)

    def step(place, _):
        slot = info[place]

        @pl.when(slot >= 0)
        def _():
            spot = coords(place)
            cut_patch(wide, spot, even, odd)
            linear = convolve(even, odd, band) + bias[...]
            keep = spread_mask(mask[slot])
            sig = sigmoid(linear)
            hidden = keep * (linear * sig)
            gates[slot] = (keep * (sig * (1.0 + linear * (1.0 - sig)))).astype(BF16)
            for j in range(4):
                piece = hidden[64 * j : 64 * j + 64].reshape(8, 8, 2 * C)
                put(vol, faces, spot, 2 * C * j, piece)

        return 0

    lax.fori_loop(0, 32, step, 0)
    put_corners(faces, corners)


def second_kernel(
    info, own, x_halo, y_halo, c_halo, mask, taps, bias, cots,
    vol, faces, corners, results, grad,
    wide, band, even, odd, sums, sems,
):
    load_volume(info, own, x_halo, y_halo, c_halo, wide, sems)
    fill_band(band, taps)
    vol[...] = jnp.zeros(vol.shape, BF16)
    faces[...] = jnp.zeros(faces.shape, BF16)
    sums[...] = jnp.zeros(sums.shape, F32)

    def step(place, _):
        slot = info[place]

        @pl.when(slot >= 0)
        def _():
            spot = coords(place)
            worker = info[36 + slot]
            cut_patch(wide, spot, even, odd)
            linear = convolve(even, odd, band) + bias[...]
            keep = spread_mask(mask[slot])
            sig = sigmoid(linear)
            output = keep * (linear * sig)
            slope = keep * (sig * (1.0 + linear * (1.0 - sig)))
            slopes = []
            for j in range(4):
                rows = slice(64 * j, 64 * j + 64)
                lanes = pl.ds(2 * C * j, 2 * C)
                results[worker, :, :, lanes] = output[rows].reshape(8, 8, 2 * C).astype(BF16)
                piece = cots[worker, :, :, lanes].astype(F32).reshape(64, 2 * C) * slope[rows]
                slopes.append(piece)
                put(vol, faces, spot, 2 * C * j, piece.reshape(8, 8, 2 * C))
            add_taps(sums, jnp.concatenate(slopes, axis=0), even, odd)

        return 0

    lax.fori_loop(0, 32, step, 0)
    put_corners(faces, corners)
    gather_taps(sums, grad)


def third_kernel(
    info, own, x_halo, y_halo, c_halo, own_in, x_halo_in, y_halo_in, c_halo_in, gates, taps,
    grad,
    wide, wide_in, band, even, odd, even_in, odd_in, sums, sems, sems_in,
):
    load_volume(info, own_in, x_halo_in, y_halo_in, c_halo_in, wide_in, sems_in)
    load_volume(info, own, x_halo, y_halo, c_halo, wide, sems)
    fill_band(band, taps)
    sums[...] = jnp.zeros(sums.shape, F32)

    def step(place, _):
        slot = info[place]

        @pl.when(slot >= 0)
        def _():
            spot = coords(place)
            cut_patch(wide, spot, even, odd)
            cut_patch(wide_in, spot, even_in, odd_in)
            back = convolve(even, odd, band)
            add_taps(sums, back * gates[slot].astype(F32), even_in, odd_in)

        return 0

    lax.fori_loop(0, 32, step, 0)
    gather_taps(sums, grad)


WIDE_SCRATCH = pltpu.VMEM((18, 4, 8, WIDE), BF16)
BAND_SCRATCH = pltpu.VMEM((9, 4 * C, 2 * C), BF16)
EVEN_SCRATCH = pltpu.VMEM((3, 80, PATCH), BF16)
ODD_SCRATCH = pltpu.VMEM((3, 64, PATCH), BF16)
SUMS_SCRATCH = pltpu.VMEM((9, 2 * C, 4 * C), F32)
SEMS = pltpu.SemaphoreType.DMA((3,))
PARAMS = pltpu.CompilerParams(vmem_limit_bytes=LIMIT)


def normalized(grad):
    return grad * lax.rsqrt(jnp.mean(grad * grad) + 1e-05)


def body(
    features,
    voxel_mask,
    occupancy,
    send_counts,
    weight_one,
    bias_one,
    weight_two,
    bias_two,
    cotangent,
):
    x, y = lax.axis_index("gx"), lax.axis_index("gy")
    nx, ny = lax.axis_size("gx"), lax.axis_size("gy")
    c_in = weight_one.shape[1]
    lanes = jnp.arange(16, dtype=jnp.int32)
    table = send_counts[0]
    outgoing = table[x]
    incoming = table[:, x]
    start = jnp.cumsum(outgoing) - outgoing
    rank = jnp.cumsum(incoming) - incoming
    hits = (start[None, :] == lanes[:, None]) & (outgoing[None, :] > 0)
    worker = jnp.sum(jnp.where(hits, lanes[None, :], 0), axis=1)
    edges = jnp.stack([x > 0, x < nx - 1, y > 0, y < ny - 1]).astype(jnp.int32)
    info = jnp.concatenate([occupancy.reshape(32), edges, worker.astype(jnp.int32)])

    cots = lax.all_to_all(
        cotangent[0, 0][jnp.minimum(rank, 7)], "gx", split_axis=0, concat_axis=0, tiled=True
    )
    mask = voxel_mask[0, 0].reshape(16, 64, 8).astype(F32)
    vol_in = pl.pallas_call(
        volume_kernel,
        out_shape=(VOLUME, FACES, CORNERS),
        in_specs=[SMEM, VMEM, VMEM],
        out_specs=(VMEM,) * 3,
        compiler_params=PARAMS,
        name="volume",
    )(info, features[0, 0], mask)
    halo_in = halo_exchange(*vol_in, 0)

    *hidden, gates = pl.pallas_call(
        first_kernel,
        out_shape=(VOLUME, FACES, CORNERS, jax.ShapeDtypeStruct((16, 256, 2 * C), BF16)),
        in_specs=[SMEM, ANY, ANY, VMEM, VMEM, VMEM, VMEM, VMEM],
        out_specs=(VMEM,) * 4,
        scratch_shapes=[WIDE_SCRATCH, BAND_SCRATCH, EVEN_SCRATCH, ODD_SCRATCH, SEMS],
        compiler_params=PARAMS,
        name="first",
    )(info, vol_in[0], *halo_in, mask, weight_one, jnp.tile(bias_one, 2)[None])
    halo_mid = halo_exchange(*hidden, 1)

    *slopes, results, grad_two = pl.pallas_call(
        second_kernel,
        out_shape=(
            VOLUME,
            FACES,
            CORNERS,
            jax.ShapeDtypeStruct((16, 8, 8, BRICK), BF16),
            jax.ShapeDtypeStruct(weight_two.shape, F32),
        ),
        in_specs=[SMEM, ANY, ANY, VMEM, VMEM, VMEM, VMEM, VMEM, VMEM],
        out_specs=(VMEM,) * 5,
        scratch_shapes=[
            WIDE_SCRATCH, BAND_SCRATCH, EVEN_SCRATCH, ODD_SCRATCH, SUMS_SCRATCH, SEMS,
        ],
        compiler_params=PARAMS,
        name="second",
    )(info, hidden[0], *halo_mid, mask, weight_two, jnp.tile(bias_two, 2)[None], cots)
    arrived = lax.all_to_all(results, "gx", split_axis=0, concat_axis=0, tiled=True)
    grad_two = lax.psum(grad_two, ("gx", "gy"))
    halo_back = halo_exchange(*slopes, 2)

    mirrored = weight_two[::-1].transpose(0, 2, 1)
    grad_one = pl.pallas_call(
        third_kernel,
        out_shape=jax.ShapeDtypeStruct(weight_one.shape, F32),
        in_specs=[SMEM, ANY, ANY, VMEM, VMEM, ANY, ANY, VMEM, VMEM, VMEM, VMEM],
        out_specs=VMEM,
        scratch_shapes=[
            WIDE_SCRATCH, WIDE_SCRATCH, BAND_SCRATCH, EVEN_SCRATCH, ODD_SCRATCH,
            EVEN_SCRATCH, ODD_SCRATCH, SUMS_SCRATCH, SEMS, SEMS,
        ],
        compiler_params=PARAMS,
        name="third",
    )(info, slopes[0], *halo_back, vol_in[0], *halo_in, gates, mirrored)
    grad_one = lax.psum(grad_one, ("gx", "gy"))

    wanted = jnp.arange(8, dtype=jnp.int32)
    from_whom = (rank[None, :] == wanted[:, None]) & (incoming[None, :] > 0)
    sender = jnp.sum(jnp.where(from_whom, lanes[None, :], 0), axis=1)
    return (arrived[sender][None, None], normalized(grad_one), normalized(grad_two))


def solution(mesh):
    placed = (
        P("gx", "gy", None, None, None, None),
        P("gx", "gy", None, None),
        P("gx", "gy", None),
        P("gy", None, None),
        P(),
        P(),
        P(),
        P(),
        P("gx", "gy", None, None, None, None),
    )
    return jax.shard_map(
        body,
        mesh=mesh,
        in_specs=placed,
        out_specs=(P("gx", "gy", None, None, None, None), P(), P()),
        check_vma=False,
    )
```

time: 1400 us -> 403 us (0.29); the launches traced: 1380 us -> 402 us
  local copies, waits for them, and re-layouts: 591 us -> 14.8 us
  waiting for transfers between devices: 426 us -> 170 us
  Pallas kernels: 0 us -> 149 us
  other arithmetic: 136 us -> 11.5 us
  starting transfers between devices: 120 us -> 41.7 us
  matrix products: 60 us -> 0 us
  loops' own time: 31.7 us -> 0 us
    gather x162 -> x2, local copies, waits for them, and re-layouts: 283 us -> 5.18 us  [the longest x1 3.17 us: body(): arrived[sender][None, None]]
    all_to_all x7 -> x2, waiting for transfers between devices: 266 us -> 0.01 us  [the longest x1 0.01 us: body(): lax.all_to_all(cotangent[0, 0][jnp.minimum(rank, 7)], 'gx', split_axis=0,...]
    pallas_call x0 -> x7, Pallas kernels: none -> 149 us  [the longest x3 90.6 us: halo_exchange(): pl.pallas_call(halo_kernel, out_shape=(jax.ShapeDtypeStruct((2, 2, 8, LIN...]
    dynamic_update_slice x16 -> x0, local copies, waits for them, and re-layouts: 92.5 us -> none  [deposit(): return lax.dynamic_update_slice(canvas, current + piece, corner)]
    conv_general_dilated x5 -> x0, matrix products: 60 us -> none  [the longest x3 34.3 us: conv_bricks(): lax.conv_general_dilated(padded, kernel, (1, 1, 1), 'VALID', dimension_nu...]
    slice x7 -> x0, local copies, waits for them, and re-layouts: 47.1 us -> none  [the longest x2 20.3 us: gradient_home(): canvas[:, :, 1:-1]]
    unnamed x51 -> x15, local copies, waits for them, and re-layouts: 45.1 us -> 3.04 us
    select_n x18 -> x1, other arithmetic: 40.4 us -> 0.01 us  [body(): arrived[sender][None, None]]
  transfers between devices with their start and end apart: 20 -> 3, of which waited for: 10 -> 1; matrix products, arithmetic and copies ran while one was open for 16% -> 5% of each run, Pallas kernels for 0% -> 16%
where the time goes in v1:
time: 403 us; the launch traced here: 402 us
  waiting for transfers between devices  170 us (42%)
  Pallas kernels  149 us (37%)
  starting transfers between devices  41.7 us (10%)
  between operations  15.6 us (4%)
  local copies, waits for them, and re-layouts  14.8 us (4%)
  other arithmetic  11.5 us (3%)
    psum x1, waiting for transfers between devices, body(): grad_one = lax.psum(grad_one, ('gx', 'gy'))  170 us
    pallas_call x3, Pallas kernels, halo_exchange(): pl.pallas_call(halo_kernel, out_shape=(jax.ShapeDtypeStruct((2, 2, 8, LIN...  90.6 us
    all_to_all x1, starting transfers between devices, body(): lax.all_to_all(results, 'gx', split_axis=0, concat_axis=0, tiled=True)  33.1 us
    pallas_call x1, Pallas kernels, body(): pl.pallas_call(second_kernel, out_shape=(VOLUME, FACES, CORNERS, jax.Shap...  21 us
    pallas_call x1, Pallas kernels, body(): pl.pallas_call(third_kernel, out_shape=jax.ShapeDtypeStruct(weight_one.sh...  20.8 us
    pallas_call x1, Pallas kernels, body(): pl.pallas_call(first_kernel, out_shape=(VOLUME, FACES, CORNERS, jax.Shape...  11.4 us
    all_to_all x1, starting transfers between devices, body(): lax.all_to_all(cotangent[0, 0][jnp.minimum(rank, 7)], 'gx', split_axis=0,...  8.56 us
  transfers between devices with their start and end apart: 3, of which 1 were waited for; matrix products, arithmetic and copies ran while one was open for 5% of the time, Pallas kernels for 16%

profile of v1, /device:TPU:1, one launch (start us, length us, event | category | flops | bytes accessed | tf_op | source)
XLA Modules:
  0.0 402.1 jit_solution(15175460448635788902)
XLA Ops:
  7.2 0.0 copy-start
  7.2 1.0 dynamic-slice_reduce_fusion
  8.2 0.1 fusion.5
  8.3 0.1 copy-done
  8.4 2.0 gather_fusion
  10.4 0.0 copy-start.4
  10.4 0.0 copy-start.3
  10.4 8.6 %all-to-all-start = ((bf16[16,8,8,1024]{3,2,1,0:T(8,128)(2,1)}), bf16[16,8,8,1024]{3,2,1,0:T(8,128)(2,1)S(1)}, u32[]{:S(2)}, u32[]{:S(2)}) async-start(bf16[16,8,8,1024]{3,2,1,0:T(8,128)(2,1)} %gather_fusion), calls=%async_computation | async-start | bytes 4194304 | tf_op jit(solution)/shard_map/all_to_all | solution.py:373
  19.0 0.0 all-reduce.3.cloned.1.call-start
  19.0 0.7 fusion.4
  19.7 0.1 copy.24
  19.9 0.1 reduce
  20.0 0.0 copy-done.4
  20.0 0.1 reshape.119
  20.1 0.0 copy-done.3
  20.1 0.1 copy.25
  20.2 1.2 copy.26.mask
  21.5 2.2 copy.31
  23.7 0.1 add_convert_fusion
  23.7 0.7 bitcast_subtract_fusion
  24.4 0.7 bitcast_compare_fusion
  25.1 0.1 select_reduce_fusion
  25.2 0.7 pad_add_fusion.info
  25.9 5.4 %volume.1 = (bf16[16,2,8,8192]{3,2,1,0:T(8,128)(2,1)}, bf16[2,2,8,8192]{3,2,1,0:T(8,128)(2,1)}, bf16[4,8,1024]{2,1,0:T(8,128)(2,1)}) custom-call(s32[52]{0:T(128)} %pad_add_fusion.info, bf16[16,8,8,768]{3,2,1,0:T(8,128)(2,1)} %bitcast.24, f32[16,64,8]{2,1,0:T(8,128)} %copy.26.mask), custom_call_target="tpu_custom_call" | custom-call | tf_op jit(solution)/shard_map/volume/pallas_call | solution.py:377
  31.3 0.0 copy-start.5
  31.3 24.9 %halo.3 = (bf16[2,2,8,8192]{3,2,1,0:T(8,128)(2,1)}, bf16[2,2,8,8192]{3,2,1,0:T(8,128)(2,1)}, bf16[4,8,1024]{2,1,0:T(8,128)(2,1)}) custom-call(bf16[16,2,8,8192]{3,2,1,0:T(8,128)(2,1)} %get-tuple-element.24.vol.own.own_in, bf16[2,2,8,8192]{3,2,1,0:T(8,128)(2,1)} %get-tuple-element.25.faces, bf16[4,8,1024]{2,1,0:T(8,128)(2,1)} %get-tuple-element.26.corners), custom_call_target="tpu_custom_call" | custom-call | tf_op jit(solution)/shard_map/halo/pallas_call | solution.py:110
  56.2 0.0 copy-done.5
  56.2 0.6 tile.4
  56.8 11.4 %first.1 = (bf16[16,2,8,8192]{3,2,1,0:T(8,128)(2,1)}, bf16[2,2,8,8192]{3,2,1,0:T(8,128)(2,1)}, bf16[4,8,1024]{2,1,0:T(8,128)(2,1)}, bf16[16,256,256]{2,1,0:T(8,128)(2,1)}) custom-call(s32[52]{0:T(128)} %pad_add_fusion.info, bf16[16,2,8,8192]{3,2,1,0:T(8,128)(2,1)} %get-tuple-element.24.vol.own.own_in, ...), custom_call_target="tpu_custom_call" | custom-call | tf_op jit(solution)/shard_map/first/pallas_call | solution.py:387
  68.1 23.0 %halo.4 = (bf16[2,2,8,8192]{3,2,1,0:T(8,128)(2,1)}, bf16[2,2,8,8192]{3,2,1,0:T(8,128)(2,1)}, bf16[4,8,1024]{2,1,0:T(8,128)(2,1)}) custom-call(bf16[16,2,8,8192]{3,2,1,0:T(8,128)(2,1)} %get-tuple-element.30.vol.own, bf16[2,2,8,8192]{3,2,1,0:T(8,128)(2,1)} %get-tuple-element.31.faces, bf16[4,8,1024]{2,1,0:T(8,128)(2,1)} %get-tuple-element.32.corners), custom_call_target="tpu_custom_call" | custom-call | tf_op jit(solution)/shard_map/halo/pallas_call | solution.py:110
  91.1 0.0 copy-start.6
  91.2 2.2 reverse_bitcast_fusion.taps
  93.4 0.0 all-to-all-done.cots
  93.4 0.0 copy-start.1
  93.4 0.0 copy-done.6
  93.4 0.6 tile.5
  94.0 0.7 copy-done.1
  94.7 21.0 %second.1 = (bf16[16,2,8,8192]{3,2,1,0:T(8,128)(2,1)}, bf16[2,2,8,8192]{3,2,1,0:T(8,128)(2,1)}, bf16[4,8,1024]{2,1,0:T(8,128)(2,1)}, bf16[16,8,8,1024]{3,2,1,0:T(8,128)(2,1)}, f32[27,128,128]{2,1,0:T(8,128)}) custom-call(s32[52]{0:T(128)} %pad_add_fusion.info, bf16[16,2,8,8192]{3,2,1,0:T(8,128)(2,1)} %get-tuple-element.30.vol.own, ...), custom_call_target="tpu_custom_call" | custom-call | tf_op jit(solution)/shard_map/second/pallas_call | solution.py:398
  115.7 42.7 %halo.5 = (bf16[2,2,8,8192]{3,2,1,0:T(8,128)(2,1)}, bf16[2,2,8,8192]{3,2,1,0:T(8,128)(2,1)}, bf16[4,8,1024]{2,1,0:T(8,128)(2,1)}) custom-call(bf16[16,2,8,8192]{3,2,1,0:T(8,128)(2,1)} %get-tuple-element.37.vol.own, bf16[2,2,8,8192]{3,2,1,0:T(8,128)(2,1)} %get-tuple-element.38.faces, bf16[4,8,1024]{2,1,0:T(8,128)(2,1)} %get-tuple-element.39.corners), custom_call_target="tpu_custom_call" | custom-call | tf_op jit(solution)/shard_map/halo/pallas_call | solution.py:110
  158.4 20.8 %third.1 = f32[27,96,128]{2,1,0:T(8,128)} custom-call(s32[52]{0:T(128)} %pad_add_fusion.info, bf16[16,2,8,8192]{3,2,1,0:T(8,128)(2,1)} %get-tuple-element.37.vol.own, bf16[2,2,8,8192]{3,2,1,0:T(8,128)(2,1)} %get-tuple-element.40.x_halo, bf16[2,2,8,8192]{3,2,1,0:T(8,128)(2,1)} %get-tuple-element.41.y_halo, bf16[4,8,1024]{2,1,0:T(8,128)(2,1)} %get-tuple-element.42.c_halo, ...), custom_call_target="tpu_custom_call" | custom-call | tf_op jit(solution)/shard_map/third/pallas_call | solution.py:420
  179.1 0.0 all-reduce.3.cloned.1.call-update
  179.2 33.1 %all-to-all-start.1 = ((bf16[16,8,8,1024]{3,2,1,0:T(8,128)(2,1)}), bf16[16,8,8,1024]{3,2,1,0:T(8,128)(2,1)}, u32[]{:S(2)}, u32[]{:S(2)}) async-start(bf16[16,8,8,1024]{3,2,1,0:T(8,128)(2,1)} %get-tuple-element.36), calls=%async_computation.1 | async-start | bytes 4194304 | tf_op jit(solution)/shard_map/all_to_all | solution.py:415
  212.2 0.1 select_reduce_fusion.1
  212.4 169.5 %all-reduce.3.cloned.1.call-done = (f32[27,96,128]{2,1,0:T(8,128)}, f32[27,128,128]{2,1,0:T(8,128)}) async-done(((f32[27,96,128]{2,1,0:T(8,128)}, f32[27,128,128]{2,1,0:T(8,128)}), (f32[27,96,128]{2,1,0:T(8,128)}, f32[27,128,128]{2,1,0:T(8,128)})) %all-reduce.3.cloned.1.call-update) | async-done | bytes 3096592 | tf_op jit(solution)/shard_map/psum | solution.py:432
  381.9 2.5 multiply_reduce_fusion
  385.1 0.0 copy-start.2
  385.1 2.4 multiply_reduce_fusion.1
  388.2 2.5 broadcast_multiply_fusion.1
  390.7 0.0 copy-done.2
  390.7 1.3 broadcast_multiply_fusion
  392.1 0.0 all-to-all-done.1
  392.1 3.2 gather_fusion.1
  (7 shorter events, 0.1 us)
Async XLA Ops:
  7.2 1.2 copy-start
  10.4 9.6 %copy-start.4 = (s32[2,2,8]{2,1,0:T(2,128)S(1)}, s32[2,2,8]{2,1,0:T(2,128)}, u32[]{:S(2)}) copy-start(s32[2,2,8]{2,1,0:T(2,128)} %param.11) | copy-start | bytes 388
  10.4 9.7 %copy-start.3 = (s32[1,1,16,512]{3,2,1,0:T(8,128)S(1)}, s32[1,1,16,512]{3,2,1,0:T(8,128)}, u32[]{:S(2)}) copy-start(s32[1,1,16,512]{3,2,1,0:T(8,128)} %param.10) | copy-start | bytes 98308
  10.4 82.9 %all-to-all-start = ((bf16[16,8,8,1024]{3,2,1,0:T(8,128)(2,1)}), bf16[16,8,8,1024]{3,2,1,0:T(8,128)(2,1)S(1)}, u32[]{:S(2)}, u32[]{:S(2)}) async-start(bf16[16,8,8,1024]{3,2,1,0:T(8,128)(2,1)} %gather_fusion), calls=%async_computation | async-start | bytes 4194304 | tf_op jit(solution)/shard_map/all_to_all | solution.py:373
  19.0 362.9 %all-reduce.3.cloned.1.call-start = ((), (), s32[]{:S(2)}) async-start(), calls=%async_computation.2 | async-start | bytes 6193152 | tf_op jit(solution)/shard_map/psum | solution.py:432
  31.3 24.9 %copy-start.5 = (f32[128]{0:T(128)S(1)}, f32[128]{0:T(128)}, u32[]{:S(2)}) copy-start(f32[128]{0:T(128)} %param.14) | copy-start | bytes 1540
  91.1 2.2 copy-start.6
  93.4 1.4 copy-start.1
  179.2 212.9 %all-to-all-start.1 = ((bf16[16,8,8,1024]{3,2,1,0:T(8,128)(2,1)}), bf16[16,8,8,1024]{3,2,1,0:T(8,128)(2,1)}, u32[]{:S(2)}, u32[]{:S(2)}) async-start(bf16[16,8,8,1024]{3,2,1,0:T(8,128)(2,1)} %get-tuple-element.36), calls=%async_computation.1 | async-start | bytes 4194304 | tf_op jit(solution)/shard_map/all_to_all | solution.py:415
  385.1 5.6 %copy-start.2 = (f32[27,128,128]{2,1,0:T(8,128)S(1)}, f32[27,128,128]{2,1,0:T(8,128)}, u32[]{:S(2)}) copy-start(f32[27,128,128]{2,1,0:T(8,128)} %get-tuple-element.48) | copy-start | bytes 5308420
Sparse Core Ops, SparseCore 0:
  179.3 202.5 all-reduce.2

commit v2 on v1

--- a/solution.py
+++ b/solution.py
@@ -10,6 +10,7 @@
 MESH = pl.DeviceIdType.MESH
 F32 = jnp.float32
 BF16 = jnp.bfloat16
+GROUP = 2
 C = 128
 BRICK = 8 * C
 LINE = 8 * BRICK
@@ -47,7 +48,15 @@
             corners[2 * side_y + side_x] = jnp.concatenate(rows, axis=0).astype(BF16)
 
 
-def volume_kernel(info, feat, mask, vol, faces, corners):
+def volume_kernel(info, feat, mask, vol, faces, corners, order):
+    def sort(place, counts):
+        active, empty = counts
+        live = info[place] >= 0
+        order[jnp.where(live, active, 31 - empty)] = place
+        one = live.astype(jnp.int32)
+        return active + one, empty + 1 - one
+
+    order[32] = lax.fori_loop(0, 32, sort, (0, 0))[0]
     vol[...] = jnp.zeros(vol.shape, BF16)
     faces[...] = jnp.zeros(faces.shape, BF16)
     c_in = feat.shape[3] // 8
@@ -175,9 +184,10 @@
 
 def window(even, odd, a, b):
     parts = []
-    for j in range(4):
-        lanes = pl.ds(2 * C * j, 4 * C)
-        parts.append(odd[b, :, lanes] if a == 1 else even[b, pl.ds(8 * a, 64), lanes])
+    for g in range(GROUP):
+        for j in range(4):
+            lanes = pl.ds(2 * C * j, 4 * C)
+            parts.append(odd[g, b, :, lanes] if a == 1 else even[g, b, pl.ds(8 * a, 64), lanes])
     return jnp.concatenate(parts, axis=0)
 
 
@@ -191,7 +201,7 @@
 
 
 def convolve(even, odd, band):
-    total = jnp.zeros((256, 2 * C), F32)
+    total = jnp.zeros((GROUP * 256, 2 * C), F32)
     for a in range(3):
         for b in range(3):
             total = total + jnp.dot(
@@ -201,7 +211,7 @@
 
 
 def add_taps(sums, slopes, even, odd):
-    turned = slopes.T.astype(BF16)
+    turned = slopes.astype(F32).T.astype(BF16)
     for a in range(3):
         for b in range(3):
             sums[3 * a + b] += jnp.dot(
@@ -209,15 +219,28 @@
             )
 
 
-def gather_taps(sums, grad):
-    depth = grad.shape[1]
+def gather_taps(sums, grad, depth):
     for tap in range(9):
         for c in range(3):
             part = (
                 sums[tap, 0:C, c * C : (c + 1) * C]
                 + sums[tap, C : 2 * C, (c + 1) * C : (c + 2) * C]
             )
-            grad[3 * tap + c] = part.T[0:depth]
+            grad[pl.ds((3 * tap + c) * depth, depth)] = part.T[0:depth].astype(BF16)
+
+
+def groups(info, order, act):
+    def step(number, _):
+        members = []
+        for g in range(GROUP):
+            position = number * GROUP + g
+            place = order[position]
+            slot = info[place]
+            members.append((position, place, jnp.maximum(slot, 0), slot >= 0))
+        act(number, members)
+        return 0
+
+    lax.fori_loop(0, (order[32] + GROUP - 1) // GROUP, step, 0)
 
 
 def spread_mask(keep):
@@ -233,7 +256,7 @@
 
 
 def first_kernel(
-    info, own, x_halo, y_halo, c_halo, mask, taps, bias,
+    info, order, own, x_halo, y_halo, c_halo, mask, taps, bias,
     vol, faces, corners, gates,
     wide, band, even, odd, sems,
 ):
@@ -242,32 +265,28 @@
     vol[...] = jnp.zeros(vol.shape, BF16)
     faces[...] = jnp.zeros(faces.shape, BF16)
 
-    def step(place, _):
-        slot = info[place]
-
-        @pl.when(slot >= 0)
-        def _():
-            spot = coords(place)
-            cut_patch(wide, spot, even, odd)
-            linear = convolve(even, odd, band) + bias[...]
-            keep = spread_mask(mask[slot])
+    def forward(number, members):
+        for g, (_, place, _, _) in enumerate(members):
+            cut_patch(wide, coords(place), even.at[g], odd.at[g])
+        both = convolve(even, odd, band) + bias[...]
+        for g, (position, place, slot, live) in enumerate(members):
+            linear = both[256 * g : 256 * g + 256]
+            keep = jnp.where(live, spread_mask(mask[slot]), 0.0)
             sig = sigmoid(linear)
             hidden = keep * (linear * sig)
-            gates[slot] = (keep * (sig * (1.0 + linear * (1.0 - sig)))).astype(BF16)
+            gates[position] = (keep * (sig * (1.0 + linear * (1.0 - sig)))).astype(BF16)
             for j in range(4):
                 piece = hidden[64 * j : 64 * j + 64].reshape(8, 8, 2 * C)
-                put(vol, faces, spot, 2 * C * j, piece)
-
-        return 0
-
-    lax.fori_loop(0, 32, step, 0)
+                put(vol, faces, coords(place), 2 * C * j, piece)
+
+    groups(info, order, forward)
     put_corners(faces, corners)
 
 
 def second_kernel(
-    info, own, x_halo, y_halo, c_halo, mask, taps, bias, cots,
+    info, order, own, x_halo, y_halo, c_halo, mask, taps, bias, cots,
     vol, faces, corners, results, grad,
-    wide, band, even, odd, sums, sems,
+    wide, band, even, odd, sums, slopes, sems,
 ):
     load_volume(info, own, x_halo, y_halo, c_halo, wide, sems)
     fill_band(band, taps)
@@ -275,74 +294,181 @@
     faces[...] = jnp.zeros(faces.shape, BF16)
     sums[...] = jnp.zeros(sums.shape, F32)
 
-    def step(place, _):
-        slot = info[place]
-
-        @pl.when(slot >= 0)
-        def _():
-            spot = coords(place)
+    def forward(number, members):
+        for g, (_, place, _, _) in enumerate(members):
+            cut_patch(wide, coords(place), even.at[g], odd.at[g])
+        both = convolve(even, odd, band) + bias[...]
+        for g, (position, place, slot, live) in enumerate(members):
             worker = info[36 + slot]
-            cut_patch(wide, spot, even, odd)
-            linear = convolve(even, odd, band) + bias[...]
-            keep = spread_mask(mask[slot])
+            linear = both[256 * g : 256 * g + 256]
+            keep = jnp.where(live, spread_mask(mask[slot]), 0.0)
             sig = sigmoid(linear)
             output = keep * (linear * sig)
             slope = keep * (sig * (1.0 + linear * (1.0 - sig)))
-            slopes = []
             for j in range(4):
                 rows = slice(64 * j, 64 * j + 64)
                 lanes = pl.ds(2 * C * j, 2 * C)
-                results[worker, :, :, lanes] = output[rows].reshape(8, 8, 2 * C).astype(BF16)
                 piece = cots[worker, :, :, lanes].astype(F32).reshape(64, 2 * C) * slope[rows]
-                slopes.append(piece)
-                put(vol, faces, spot, 2 * C * j, piece.reshape(8, 8, 2 * C))
-            add_taps(sums, jnp.concatenate(slopes, axis=0), even, odd)
-
-        return 0
-
-    lax.fori_loop(0, 32, step, 0)
+                slopes[position, pl.ds(64 * j, 64)] = piece.astype(BF16)
+                put(vol, faces, coords(place), 2 * C * j, piece.reshape(8, 8, 2 * C))
+
+            @pl.when(live)
+            def _():
+                for j in range(4):
+                    rows = output[64 * j : 64 * j + 64].reshape(8, 8, 2 * C)
+                    results[worker, :, :, pl.ds(2 * C * j, 2 * C)] = rows.astype(BF16)
+
+    def backward(number, members):
+        for g, (_, place, _, _) in enumerate(members):
+            cut_patch(wide, coords(place), even.at[g], odd.at[g])
+        rows = slopes[pl.ds(number * GROUP, GROUP)].reshape(GROUP * 256, 2 * C)
+        add_taps(sums, rows, even, odd)
+
+    groups(info, order, forward)
     put_corners(faces, corners)
-    gather_taps(sums, grad)
+    groups(info, order, backward)
+    gather_taps(sums, grad, C)
 
 
 def third_kernel(
-    info, own, x_halo, y_halo, c_halo, own_in, x_halo_in, y_halo_in, c_halo_in, gates, taps,
-    grad,
-    wide, wide_in, band, even, odd, even_in, odd_in, sums, sems, sems_in,
+    info, order, own, x_halo, y_halo, c_halo, own_in, x_halo_in, y_halo_in, c_halo_in, gates,
+    taps, grad_two, c_in,
+    grads,
+    wide, wide_in, band, even, odd, sums, slopes, sems, sems_in,
 ):
     load_volume(info, own_in, x_halo_in, y_halo_in, c_halo_in, wide_in, sems_in)
     load_volume(info, own, x_halo, y_halo, c_halo, wide, sems)
     fill_band(band, taps)
     sums[...] = jnp.zeros(sums.shape, F32)
 
-    def step(place, _):
-        slot = info[place]
-
-        @pl.when(slot >= 0)
-        def _():
-            spot = coords(place)
-            cut_patch(wide, spot, even, odd)
-            cut_patch(wide_in, spot, even_in, odd_in)
-            back = convolve(even, odd, band)
-            add_taps(sums, back * gates[slot].astype(F32), even_in, odd_in)
-
-        return 0
-
-    lax.fori_loop(0, 32, step, 0)
-    gather_taps(sums, grad)
+    def back(number, members):
+        for g, (_, place, _, _) in enumerate(members):
+            cut_patch(wide, coords(place), even.at[g], odd.at[g])
+        both = convolve(even, odd, band)
+        for g, (position, _, _, _) in enumerate(members):
+            rows = both[256 * g : 256 * g + 256] * gates[position].astype(F32)
+            slopes[position] = rows.astype(BF16)
+
+    def backward(number, members):
+        for g, (_, place, _, _) in enumerate(members):
+            cut_patch(wide_in, coords(place), even.at[g], odd.at[g])
+        rows = slopes[pl.ds(number * GROUP, GROUP)].reshape(GROUP * 256, 2 * C)
+        add_taps(sums, rows, even, odd)
+
+    groups(info, order, back)
+    groups(info, order, backward)
+    gather_taps(sums, grads, c_in)
+    first_rows, second_rows = 27 * c_in, grad_two.shape[0]
+    grads[first_rows : first_rows + second_rows] = grad_two[...]
+    rest = grads.shape[0] - first_rows - second_rows
+    grads[first_rows + second_rows :] = jnp.zeros((rest, C), BF16)
+
+
+def reduce_kernel(
+    grads,
+    final,
+    from_core, half, parts, line, send_sem, recv_sem,
+):
+    nx, ny = lax.axis_size("gx"), lax.axis_size("gy")
+    x, y = lax.axis_index("gx"), lax.axis_index("gy")
+    core, chip = lax.rem(y, 2), y // 2
+    partner = (x, y + 1 - 2 * core)
+    across = [(lax.rem(x + k, nx), y) for k in range(1, nx)]
+    along = [(x, 2 * lax.rem(chip + k, ny // 2) + core) for k in range(1, ny // 2)]
+    count = half.shape[0]
+    chunk = count // nx
+    mine = pl.multiple_of(core * count, count)
+    others = pl.multiple_of((1 - core) * count, count)
+    kept = pl.ds(pl.multiple_of(mine + x * chunk, chunk), chunk)
+
+    barrier = pltpu.get_barrier_semaphore()
+    peers = [partner] + across + along
+    for device in peers:
+        pl.semaphore_signal(barrier, inc=1, device_id=device, device_id_type=MESH)
+    pl.semaphore_wait(barrier, len(peers))
+
+    def send(source, target, device, number):
+        copy = pltpu.make_async_remote_copy(
+            src_ref=source,
+            dst_ref=target,
+            send_sem=send_sem.at[number],
+            recv_sem=recv_sem.at[number],
+            device_id=device,
+            device_id_type=MESH,
+        )
+        copy.start()
+        return copy
+
+    send(grads.at[pl.ds(others, count)], from_core, partner, 0).wait()
+    half[...] = (grads[pl.ds(mine, count)].astype(F32) + from_core[...].astype(F32)).astype(BF16)
+
+    copies = []
+    for k, device in enumerate(across):
+        rows = pl.ds(pl.multiple_of(device[0] * chunk, chunk), chunk)
+        copies.append(send(half.at[rows], parts.at[k], device, 1 + k))
+    total = half[pl.ds(pl.multiple_of(x * chunk, chunk), chunk)].astype(F32)
+    for k, copy in enumerate(copies):
+        copy.wait()
+        total = total + parts[k].astype(F32)
+
+    line[chip] = total.astype(BF16)
+    copies = [send(line.at[chip], line.at[chip], d, nx + k) for k, d in enumerate(along)]
+    for copy in copies:
+        copy.wait()
+    total = line[0].astype(F32)
+    for k in range(1, ny // 2):
+        total = total + line[k].astype(F32)
+    final[kept] = total.astype(BF16)
+
+    first = nx + len(along)
+    copies = [send(final.at[kept], final.at[kept], d, first + k) for k, d in enumerate(across)]
+    for copy in copies:
+        copy.wait()
+    part = final.at[pl.ds(mine, count)]
+    send(part, part, partner, first + len(across)).wait()
+
+
+def reduce_grads(grads, nx, ny):
+    count = grads.shape[0] // 2
+    sems = 2 * nx + ny // 2 - 1
+    return pl.pallas_call(
+        reduce_kernel,
+        out_shape=jax.ShapeDtypeStruct(grads.shape, BF16),
+        in_specs=[VMEM],
+        out_specs=VMEM,
+        scratch_shapes=[
+            pltpu.VMEM((count, C), BF16),
+            pltpu.VMEM((count, C), BF16),
+            pltpu.VMEM((nx - 1, count // nx, C), BF16),
+            pltpu.VMEM((ny // 2, count // nx, C), BF16),
+            pltpu.SemaphoreType.DMA((sems,)),
+            pltpu.SemaphoreType.DMA((sems,)),
+        ],
+        compiler_params=pltpu.CompilerParams(
+            collective_id=3, has_side_effects=True, vmem_limit_bytes=LIMIT
+        ),
+        name="reduce",
+    )(grads)
+
+
+def finish_kernel(sender, grads, arrived, result, grad_one, grad_two):
+    for number in range(result.shape[0]):
+        result[number] = arrived[sender[number]]
+    first = 0
+    for out in (grad_one, grad_two):
+        rows = grads[first : first + out.shape[0]].astype(F32)
+        out[...] = rows * lax.rsqrt(jnp.mean(rows * rows) + 1e-05)
+        first += out.shape[0]
 
 
 WIDE_SCRATCH = pltpu.VMEM((18, 4, 8, WIDE), BF16)
 BAND_SCRATCH = pltpu.VMEM((9, 4 * C, 2 * C), BF16)
-EVEN_SCRATCH = pltpu.VMEM((3, 80, PATCH), BF16)
-ODD_SCRATCH = pltpu.VMEM((3, 64, PATCH), BF16)
+EVEN_SCRATCH = pltpu.VMEM((GROUP, 3, 80, PATCH), BF16)
+ODD_SCRATCH = pltpu.VMEM((GROUP, 3, 64, PATCH), BF16)
+SLOPES_SCRATCH = pltpu.VMEM((16, 256, 2 * C), BF16)
 SUMS_SCRATCH = pltpu.VMEM((9, 2 * C, 4 * C), F32)
 SEMS = pltpu.SemaphoreType.DMA((3,))
 PARAMS = pltpu.CompilerParams(vmem_limit_bytes=LIMIT)
-
-
-def normalized(grad):
-    return grad * lax.rsqrt(jnp.mean(grad * grad) + 1e-05)
 
 
 def body(
@@ -374,11 +500,11 @@
         cotangent[0, 0][jnp.minimum(rank, 7)], "gx", split_axis=0, concat_axis=0, tiled=True
     )
     mask = voxel_mask[0, 0].reshape(16, 64, 8).astype(F32)
-    vol_in = pl.pallas_call(
+    *vol_in, order = pl.pallas_call(
         volume_kernel,
-        out_shape=(VOLUME, FACES, CORNERS),
+        out_shape=(VOLUME, FACES, CORNERS, jax.ShapeDtypeStruct((33,), jnp.int32)),
         in_specs=[SMEM, VMEM, VMEM],
-        out_specs=(VMEM,) * 3,
+        out_specs=(VMEM, VMEM, VMEM, SMEM),
         compiler_params=PARAMS,
         name="volume",
     )(info, features[0, 0], mask)
@@ -387,12 +513,12 @@
     *hidden, gates = pl.pallas_call(
         first_kernel,
         out_shape=(VOLUME, FACES, CORNERS, jax.ShapeDtypeStruct((16, 256, 2 * C), BF16)),
-        in_specs=[SMEM, ANY, ANY, VMEM, VMEM, VMEM, VMEM, VMEM],
+        in_specs=[SMEM, SMEM, ANY, ANY, VMEM, VMEM, VMEM, VMEM, VMEM],
         out_specs=(VMEM,) * 4,
         scratch_shapes=[WIDE_SCRATCH, BAND_SCRATCH, EVEN_SCRATCH, ODD_SCRATCH, SEMS],
         compiler_params=PARAMS,
         name="first",
-    )(info, vol_in[0], *halo_in, mask, weight_one, jnp.tile(bias_one, 2)[None])
+    )(info, order, vol_in[0], *halo_in, mask, weight_one, jnp.tile(bias_one, 2)[None])
     halo_mid = halo_exchange(*hidden, 1)
 
     *slopes, results, grad_two = pl.pallas_call(
@@ -402,39 +528,58 @@
             FACES,
             CORNERS,
             jax.ShapeDtypeStruct((16, 8, 8, BRICK), BF16),
-            jax.ShapeDtypeStruct(weight_two.shape, F32),
+            jax.ShapeDtypeStruct((27 * C, C), BF16),
         ),
-        in_specs=[SMEM, ANY, ANY, VMEM, VMEM, VMEM, VMEM, VMEM, VMEM],
+        in_specs=[SMEM, SMEM, ANY, ANY, VMEM, VMEM, VMEM, VMEM, VMEM, VMEM],
         out_specs=(VMEM,) * 5,
         scratch_shapes=[
-            WIDE_SCRATCH, BAND_SCRATCH, EVEN_SCRATCH, ODD_SCRATCH, SUMS_SCRATCH, SEMS,
+            WIDE_SCRATCH, BAND_SCRATCH, EVEN_SCRATCH, ODD_SCRATCH, SUMS_SCRATCH,
+            SLOPES_SCRATCH, SEMS,
         ],
         compiler_params=PARAMS,
         name="second",
-    )(info, hidden[0], *halo_mid, mask, weight_two, jnp.tile(bias_two, 2)[None], cots)
+    )(info, order, hidden[0], *halo_mid, mask, weight_two, jnp.tile(bias_two, 2)[None], cots)
+    halo_back = halo_exchange(*slopes, 2)
+    halo_back, results = lax.optimization_barrier((halo_back, results))
     arrived = lax.all_to_all(results, "gx", split_axis=0, concat_axis=0, tiled=True)
-    grad_two = lax.psum(grad_two, ("gx", "gy"))
-    halo_back = halo_exchange(*slopes, 2)
 
     mirrored = weight_two[::-1].transpose(0, 2, 1)
-    grad_one = pl.pallas_call(
-        third_kernel,
-        out_shape=jax.ShapeDtypeStruct(weight_one.shape, F32),
-        in_specs=[SMEM, ANY, ANY, VMEM, VMEM, ANY, ANY, VMEM, VMEM, VMEM, VMEM],
+    blocks = (27 * (c_in + C) // 16 + nx * ny - 1) // (nx * ny)
+    grads = pl.pallas_call(
+        lambda *refs: third_kernel(*refs[:13], c_in, *refs[13:]),
+        out_shape=jax.ShapeDtypeStruct((16 * nx * ny * blocks, C), BF16),
+        in_specs=[SMEM, SMEM, ANY, ANY, VMEM, VMEM, ANY, ANY, VMEM, VMEM, VMEM, VMEM, VMEM],
         out_specs=VMEM,
         scratch_shapes=[
-            WIDE_SCRATCH, WIDE_SCRATCH, BAND_SCRATCH, EVEN_SCRATCH, ODD_SCRATCH,
-            EVEN_SCRATCH, ODD_SCRATCH, SUMS_SCRATCH, SEMS, SEMS,
+            WIDE_SCRATCH, WIDE_SCRATCH, BAND_SCRATCH, EVEN_SCRATCH, ODD_SCRATCH, SUMS_SCRATCH,
+            SLOPES_SCRATCH, SEMS, SEMS,
         ],
         compiler_params=PARAMS,
+        cost_estimate=pl.CostEstimate(flops=33 * 10**9, bytes_accessed=10**8, transcendentals=0),
         name="third",
-    )(info, slopes[0], *halo_back, vol_in[0], *halo_in, gates, mirrored)
-    grad_one = lax.psum(grad_one, ("gx", "gy"))
+    )(info, order, slopes[0], *halo_back, vol_in[0], *halo_in, gates, mirrored, grad_two)
+    grads = reduce_grads(grads, nx, ny)
 
     wanted = jnp.arange(8, dtype=jnp.int32)
     from_whom = (rank[None, :] == wanted[:, None]) & (incoming[None, :] > 0)
     sender = jnp.sum(jnp.where(from_whom, lanes[None, :], 0), axis=1)
-    return (arrived[sender][None, None], normalized(grad_one), normalized(grad_two))
+    result, grad_one, grad_two = pl.pallas_call(
+        finish_kernel,
+        out_shape=(
+            jax.ShapeDtypeStruct((8, 8, 8, BRICK), BF16),
+            jax.ShapeDtypeStruct((27 * c_in, C), F32),
+            jax.ShapeDtypeStruct((27 * C, C), F32),
+        ),
+        in_specs=[SMEM, VMEM, VMEM],
+        out_specs=(VMEM,) * 3,
+        compiler_params=PARAMS,
+        name="finish",
+    )(sender, grads, arrived)
+    return (
+        result[None, None],
+        grad_one.reshape(weight_one.shape),
+        grad_two.reshape(weight_two.shape),
+    )
 
 
 def solution(mesh):

time: 403 us -> 219 us (0.54)
  waiting for transfers between devices: 170 us -> 0.01 us
  Pallas kernels: 149 us -> 189 us
  starting transfers between devices: 41.7 us -> 12.5 us
  between operations: 15.6 us -> 0.83 us
  other arithmetic: 11.5 us -> 3.16 us
    psum x1 -> x0, waiting for transfers between devices: 170 us -> none  [body(): grad_one = lax.psum(grad_one, ('gx', 'gy'))]
    pallas_call x2 -> x4, Pallas kernels: 26.1 us -> 86.3 us  [the longest x1 51 us: reduce_grads(): pl.pallas_call(reduce_kernel, out_shape=jax.ShapeDtypeStruct(grads.shape,...]
    all_to_all x1, starting transfers between devices: 33.1 us -> 3.91 us  [body(): lax.all_to_all(results, 'gx', split_axis=0, concat_axis=0, tiled=True)]
    pallas_call x3, Pallas kernels: 90.6 us -> 62.1 us  [halo_exchange(): pl.pallas_call(halo_kernel, out_shape=(jax.ShapeDtypeStruct((2, 2, 8, LIN...]
    reduce_sum x2 -> x0, other arithmetic: 4.93 us -> none  [normalized(): return grad * lax.rsqrt(jnp.mean(grad * grad) + 1e-05)]
    pallas_call x1, Pallas kernels: 11.4 us -> 15.5 us  [body(): pl.pallas_call(first_kernel, out_shape=(VOLUME, FACES, CORNERS, jax.Shape...]
  transfers between devices with their start and end apart: 3 -> 2, of which waited for: 1 -> 0; matrix products, arithmetic and copies ran while one was open for 5% -> 5% of each run, Pallas kernels for 16% -> 63%
where the time goes in v2:
time: 219 us; the launch traced here: 218 us
  Pallas kernels  189 us (86%)
  local copies, waits for them, and re-layouts  13 us (6%)
  starting transfers between devices  12.5 us (6%)
  other arithmetic  3.16 us (1%)
    pallas_call x3, Pallas kernels, halo_exchange(): pl.pallas_call(halo_kernel, out_shape=(jax.ShapeDtypeStruct((2, 2, 8, LIN...  62.1 us
    pallas_call x1, Pallas kernels, reduce_grads(): pl.pallas_call(reduce_kernel, out_shape=jax.ShapeDtypeStruct(grads.shape,...  51 us
    pallas_call x1, Pallas kernels, body(): pl.pallas_call(second_kernel, out_shape=(VOLUME, FACES, CORNERS, jax.Shap...  24.9 us
    pallas_call x1, Pallas kernels, body(): pl.pallas_call(lambda *refs: third_kernel(*refs[:13], c_in, *refs[13:]),...  23.8 us
    pallas_call x1, Pallas kernels, body(): pl.pallas_call(first_kernel, out_shape=(VOLUME, FACES, CORNERS, jax.Shape...  15.5 us
    all_to_all x1, starting transfers between devices, body(): lax.all_to_all(cotangent[0, 0][jnp.minimum(rank, 7)], 'gx', split_axis=0,...  8.56 us
    pallas_call x1, Pallas kernels, body(): pl.pallas_call(volume_kernel, out_shape=(VOLUME, FACES, CORNERS, jax.Shap...  6.9 us
    pallas_call x1, Pallas kernels, body(): pl.pallas_call(finish_kernel, out_shape=(jax.ShapeDtypeStruct((8, 8, 8, B...  4.59 us
  transfers between devices with their start and end apart: 2, of which 0 were waited for; matrix products, arithmetic and copies ran while one was open for 5% of the time, Pallas kernels for 63%

profile of v2, /device:TPU:1, one launch (start us, length us, event | category | flops | bytes accessed | tf_op | source)
XLA Modules:
  0.0 218.3 jit_solution(1807931975068260539)
XLA Ops:
  0.6 0.0 copy-start
  0.7 1.0 dynamic-slice_reduce_fusion
  1.7 0.1 fusion
  1.8 0.1 copy-done
  1.9 2.0 gather_fusion
  3.9 0.0 copy-start.4
  3.9 0.0 copy-start.3
  3.9 8.6 %all-to-all-start = ((bf16[16,8,8,1024]{3,2,1,0:T(8,128)(2,1)}), bf16[16,8,8,1024]{3,2,1,0:T(8,128)(2,1)S(1)}, u32[]{:S(2)}, u32[]{:S(2)}) async-start(bf16[16,8,8,1024]{3,2,1,0:T(8,128)(2,1)} %gather_fusion), calls=%async_computation | async-start | bytes 4194304 | tf_op jit(solution)/shard_map/all_to_all | solution.py:499
  12.5 0.7 fusion.3
  13.2 0.1 copy.25
  13.3 0.1 reduce.3
  13.4 0.0 copy-done.4
  13.4 0.1 reshape.114
  13.5 0.0 copy-done.3
  13.5 0.1 copy.26
  13.6 1.2 copy.27.mask
  14.9 2.2 %copy.31 = bf16[27,128,128]{1,2,0:T(8,128)(2,1)} copy(bf16[27,128,128]{2,1,0:T(8,128)(2,1)} %taps.3) | data formatting | bytes 1769472 | tf_op args[6]
  17.1 0.7 bitcast_compare_fusion
  17.8 0.1 add_convert_fusion
  17.9 0.7 bitcast_subtract_fusion
  18.5 0.1 select_reduce_fusion
  18.7 0.6 pad_add_fusion.info.refs_0_
  19.3 6.9 %volume.1 = (bf16[16,2,8,8192]{3,2,1,0:T(8,128)(2,1)}, bf16[2,2,8,8192]{3,2,1,0:T(8,128)(2,1)}, bf16[4,8,1024]{2,1,0:T(8,128)(2,1)}, s32[33]{0:T(128)}) custom-call(s32[52]{0:T(128)} %pad_add_fusion.info.refs_0_, bf16[16,8,8,768]{3,2,1,0:T(8,128)(2,1)} %bitcast.22, f32[16,64,8]{2,1,0:T(8,128)} %copy.27.mask), custom_call_target="tpu_custom_call" | custom-call | tf_op jit(solution)/shard_map/volume/pallas_call | solution.py:503
  26.2 0.0 copy-start.5
  26.2 23.4 %halo.3 = (bf16[2,2,8,8192]{3,2,1,0:T(8,128)(2,1)}, bf16[2,2,8,8192]{3,2,1,0:T(8,128)(2,1)}, bf16[4,8,1024]{2,1,0:T(8,128)(2,1)}) custom-call(bf16[16,2,8,8192]{3,2,1,0:T(8,128)(2,1)} %get-tuple-element.33.vol.own.refs_6_, bf16[2,2,8,8192]{3,2,1,0:T(8,128)(2,1)} %get-tuple-element.34.faces, bf16[4,8,1024]{2,1,0:T(8,128)(2,1)} %get-tuple-element.35.corners), custom_call_target="tpu_custom_call" | custom-call | tf_op jit(solution)/shard_map/halo/pallas_call | solution.py:119
  49.5 0.0 copy-done.5
  49.6 0.6 tile.4
  50.1 15.5 %first.1 = (bf16[16,2,8,8192]{3,2,1,0:T(8,128)(2,1)}, bf16[2,2,8,8192]{3,2,1,0:T(8,128)(2,1)}, bf16[4,8,1024]{2,1,0:T(8,128)(2,1)}, bf16[16,256,256]{2,1,0:T(8,128)(2,1)}) custom-call(s32[52]{0:T(128)} %pad_add_fusion.info.refs_0_, s32[33]{0:T(128)} %get-tuple-element.32.order.refs_1_, bf16[16,2,8,8192]{3,2,1,0:T(8,128)(2,1)} %get-tuple-element.33.vol.own.refs_6_, ...), custom_call_target="tpu_custom_call" | custom-call | tf_op jit(solution)/shard_map/first/pallas_call | solution.py:513
  65.6 0.0 copy-start.6
  65.7 16.4 %halo.4 = (bf16[2,2,8,8192]{3,2,1,0:T(8,128)(2,1)}, bf16[2,2,8,8192]{3,2,1,0:T(8,128)(2,1)}, bf16[4,8,1024]{2,1,0:T(8,128)(2,1)}) custom-call(bf16[16,2,8,8192]{3,2,1,0:T(8,128)(2,1)} %get-tuple-element.39.vol.own, bf16[2,2,8,8192]{3,2,1,0:T(8,128)(2,1)} %get-tuple-element.40.faces, bf16[4,8,1024]{2,1,0:T(8,128)(2,1)} %get-tuple-element.41.corners), custom_call_target="tpu_custom_call" | custom-call | tf_op jit(solution)/shard_map/halo/pallas_call | solution.py:119
  82.1 0.6 select_reduce_fusion.1.sender
  82.8 2.2 reverse_bitcast_fusion.refs_11_
  84.9 0.0 all-to-all-done.cots
  84.9 0.0 copy-start.1
  84.9 0.0 copy-done.6
  85.0 0.6 tile.5
  85.6 0.7 copy-done.1
  86.3 24.9 %second.1 = (bf16[16,2,8,8192]{3,2,1,0:T(8,128)(2,1)}, bf16[2,2,8,8192]{3,2,1,0:T(8,128)(2,1)}, bf16[4,8,1024]{2,1,0:T(8,128)(2,1)}, bf16[16,8,8,1024]{3,2,1,0:T(8,128)(2,1)}, bf16[3456,128]{1,0:T(8,128)(2,1)}) custom-call(s32[52]{0:T(128)} %pad_add_fusion.info.refs_0_, s32[33]{0:T(128)} %get-tuple-element.32.order.refs_1_, ...), custom_call_target="tpu_custom_call" | custom-call | tf_op jit(solution)/shard_map/second/pallas_call | solution.py:524
  111.2 22.3 %halo.5 = (bf16[2,2,8,8192]{3,2,1,0:T(8,128)(2,1)}, bf16[2,2,8,8192]{3,2,1,0:T(8,128)(2,1)}, bf16[4,8,1024]{2,1,0:T(8,128)(2,1)}) custom-call(bf16[16,2,8,8192]{3,2,1,0:T(8,128)(2,1)} %get-tuple-element.45.vol.refs_2_, bf16[2,2,8,8192]{3,2,1,0:T(8,128)(2,1)} %get-tuple-element.46.faces, bf16[4,8,1024]{2,1,0:T(8,128)(2,1)} %get-tuple-element.47.corners), custom_call_target="tpu_custom_call" | custom-call | tf_op jit(solution)/shard_map/halo/pallas_call | solution.py:119
  133.5 3.9 %all-to-all-start.1 = ((bf16[16,8,8,1024]{3,2,1,0:T(8,128)(2,1)}), bf16[16,8,8,1024]{3,2,1,0:T(8,128)(2,1)S(1)}, u32[]{:S(2)}, u32[]{:S(2)}) async-start(bf16[16,8,8,1024]{3,2,1,0:T(8,128)(2,1)} %get-tuple-element.57), calls=%async_computation.1 | async-start | bytes 4194304 | tf_op jit(solution)/shard_map/all_to_all | solution.py:544
  137.4 23.8 %third.1.grads = bf16[6144,128]{1,0:T(8,128)(2,1)} custom-call(s32[52]{0:T(128)} %pad_add_fusion.info.refs_0_, s32[33]{0:T(128)} %get-tuple-element.32.order.refs_1_, bf16[16,2,8,8192]{3,2,1,0:T(8,128)(2,1)} %get-tuple-element.45.vol.refs_2_, bf16[2,2,8,8192]{3,2,1,0:T(8,128)(2,1)} %get-tuple-element.52.refs_3_, ...), custom_call_target="tpu_custom_call" | custom-call | flops 32999999488 | bytes 100000000 | tf_op jit(solution)/shard_map/third/pallas_call | solution.py:548
  161.3 51.0 %reduce.8.grads = bf16[6144,128]{1,0:T(8,128)(2,1)} custom-call(bf16[6144,128]{1,0:T(8,128)(2,1)} %third.1.grads), custom_call_target="tpu_custom_call" | custom-call | tf_op jit(solution)/shard_map/reduce/pallas_call | solution.py:434
  212.3 0.0 all-to-all-done.1.arrived
  212.3 0.0 copy-start.2
  212.3 1.3 copy-done.2
  213.7 4.6 %finish.1 = (bf16[8,8,8,1024]{3,2,1,0:T(8,128)(2,1)}, f32[2592,128]{1,0:T(8,128)}, f32[3456,128]{1,0:T(8,128)}) custom-call(s32[8]{0:T(128)} %select_reduce_fusion.1.sender, bf16[6144,128]{1,0:T(8,128)(2,1)} %reduce.8.grads, bf16[16,8,8,1024]{3,2,1,0:T(8,128)(2,1)} %copy-done.2), custom_call_target="tpu_custom_call" | custom-call | tf_op jit(solution)/shard_map/finish/pallas_call | solution.py:566
  (6 shorter events, 0.1 us)
Async XLA Ops:
  0.6 1.2 copy-start
  3.9 9.5 %copy-start.4 = (s32[2,2,8]{2,1,0:T(2,128)S(1)}, s32[2,2,8]{2,1,0:T(2,128)}, u32[]{:S(2)}) copy-start(s32[2,2,8]{2,1,0:T(2,128)} %param.11) | copy-start | bytes 388
  3.9 9.6 %copy-start.3 = (s32[1,1,16,512]{3,2,1,0:T(8,128)S(1)}, s32[1,1,16,512]{3,2,1,0:T(8,128)}, u32[]{:S(2)}) copy-start(s32[1,1,16,512]{3,2,1,0:T(8,128)} %param.10) | copy-start | bytes 98308
  3.9 81.1 %all-to-all-start = ((bf16[16,8,8,1024]{3,2,1,0:T(8,128)(2,1)}), bf16[16,8,8,1024]{3,2,1,0:T(8,128)(2,1)S(1)}, u32[]{:S(2)}, u32[]{:S(2)}) async-start(bf16[16,8,8,1024]{3,2,1,0:T(8,128)(2,1)} %gather_fusion), calls=%async_computation | async-start | bytes 4194304 | tf_op jit(solution)/shard_map/all_to_all | solution.py:499
  26.2 23.4 %copy-start.5 = (f32[128]{0:T(128)S(1)}, f32[128]{0:T(128)}, u32[]{:S(2)}) copy-start(f32[128]{0:T(128)} %param.14) | copy-start | bytes 1540
  65.6 19.3 %copy-start.6 = (f32[128]{0:T(128)S(1)}, f32[128]{0:T(128)}, u32[]{:S(2)}) copy-start(f32[128]{0:T(128)} %param.16) | copy-start | bytes 1540
  84.9 1.4 copy-start.1
  133.5 78.8 %all-to-all-start.1 = ((bf16[16,8,8,1024]{3,2,1,0:T(8,128)(2,1)}), bf16[16,8,8,1024]{3,2,1,0:T(8,128)(2,1)S(1)}, u32[]{:S(2)}, u32[]{:S(2)}) async-start(bf16[16,8,8,1024]{3,2,1,0:T(8,128)(2,1)} %get-tuple-element.57), calls=%async_computation.1 | async-start | bytes 4194304 | tf_op jit(solution)/shard_map/all_to_all | solution.py:544
  212.3 1.4 copy-start.2

commit v3 on v2

--- a/solution.py
+++ b/solution.py
@@ -48,15 +48,36 @@
             corners[2 * side_y + side_x] = jnp.concatenate(rows, axis=0).astype(BF16)
 
 
-def volume_kernel(info, feat, mask, vol, faces, corners, order):
-    def sort(place, counts):
-        active, empty = counts
-        live = info[place] >= 0
+def volume_kernel(
+    occupancy, counts, feat, mask, cotangent,
+    vol, faces, corners, cots, info, order, sender,
+):
+    x, y = lax.axis_index("gx"), lax.axis_index("gy")
+    info[32] = (x > 0).astype(jnp.int32)
+    info[33] = (x < lax.axis_size("gx") - 1).astype(jnp.int32)
+    info[34] = (y > 0).astype(jnp.int32)
+    info[35] = (y < lax.axis_size("gy") - 1).astype(jnp.int32)
+
+    def sort(place, numbers):
+        active, empty = numbers
+        xb, yb, zb = coords(place)
+        slot = occupancy[xb, yb, zb]
+        info[place] = slot
+        live = slot >= 0
         order[jnp.where(live, active, 31 - empty)] = place
         one = live.astype(jnp.int32)
         return active + one, empty + 1 - one
 
     order[32] = lax.fori_loop(0, 32, sort, (0, 0))[0]
+
+    def route(peer, numbers):
+        slot, brick = numbers
+        info[36 + slot] = peer
+        sender[brick] = peer
+        cots[peer] = cotangent[jnp.minimum(brick, 7)]
+        return slot + counts[0, x, peer], brick + counts[0, peer, x]
+
+    lax.fori_loop(0, 16, route, (0, 0))
     vol[...] = jnp.zeros(vol.shape, BF16)
     faces[...] = jnp.zeros(faces.shape, BF16)
     c_in = feat.shape[3] // 8
@@ -191,13 +212,14 @@
     return jnp.concatenate(parts, axis=0)
 
 
-def fill_band(band, taps):
+def fill_band(band, taps, mirrored=False):
     depth = taps.shape[1]
     band[...] = jnp.zeros(band.shape, BF16)
     for tap in range(9):
         for c in range(3):
+            block = taps[26 - 3 * tap - c].T if mirrored else taps[3 * tap + c]
             for o in range(2):
-                band[tap, pl.ds((c + o) * C, depth), pl.ds(o * C, C)] = taps[3 * tap + c]
+                band[tap, pl.ds((c + o) * C, depth), pl.ds(o * C, C)] = block
 
 
 def convolve(even, odd, band):
@@ -338,7 +360,7 @@
 ):
     load_volume(info, own_in, x_halo_in, y_halo_in, c_halo_in, wide_in, sems_in)
     load_volume(info, own, x_halo, y_halo, c_halo, wide, sems)
-    fill_band(band, taps)
+    fill_band(band, taps, mirrored=True)
     sums[...] = jnp.zeros(sums.shape, F32)
 
     def back(number, members):
@@ -367,27 +389,39 @@
 def reduce_kernel(
     grads,
     final,
-    from_core, half, parts, line, send_sem, recv_sem,
+    from_core, half, got_1, sum_1, got_2, sum_2, got_3, send_sem, recv_sem,
 ):
-    nx, ny = lax.axis_size("gx"), lax.axis_size("gy")
     x, y = lax.axis_index("gx"), lax.axis_index("gy")
-    core, chip = lax.rem(y, 2), y // 2
+    core = lax.rem(y, 2)
+    spot = {"x": x // 4, "z": lax.rem(x, 4), "y": y // 2}
     partner = (x, y + 1 - 2 * core)
-    across = [(lax.rem(x + k, nx), y) for k in range(1, nx)]
-    along = [(x, 2 * lax.rem(chip + k, ny // 2) + core) for k in range(1, ny // 2)]
+
+    def peer(axis, k):
+        at = lax.rem(spot[axis] + k, 4)
+        if axis == "x":
+            return at, (4 * at + spot["z"], y)
+        if axis == "z":
+            return at, (4 * spot["x"] + at, y)
+        return at, (x, 2 * at + core)
+
     count = half.shape[0]
-    chunk = count // nx
+    part = count // 3
+    size_1, size_2, size_3 = part // 4, part // 16, part // 64
     mine = pl.multiple_of(core * count, count)
     others = pl.multiple_of((1 - core) * count, count)
-    kept = pl.ds(pl.multiple_of(mine + x * chunk, chunk), chunk)
+    axes = [("x", "z", "y"), ("z", "y", "x"), ("y", "x", "z")]
+    steps = range(1, 4)
 
     barrier = pltpu.get_barrier_semaphore()
-    peers = [partner] + across + along
-    for device in peers:
+    everyone = [partner] + [peer(axis, k)[1] for axis in "xyz" for k in steps]
+    for device in everyone:
         pl.semaphore_signal(barrier, inc=1, device_id=device, device_id_type=MESH)
-    pl.semaphore_wait(barrier, len(peers))
-
-    def send(source, target, device, number):
+    pl.semaphore_wait(barrier, len(everyone))
+
+    used = iter(range(send_sem.shape[0]))
+
+    def send(source, target, device):
+        number = next(used)
         copy = pltpu.make_async_remote_copy(
             src_ref=source,
             dst_ref=target,
@@ -399,38 +433,83 @@
         copy.start()
         return copy
 
-    send(grads.at[pl.ds(others, count)], from_core, partner, 0).wait()
-    half[...] = (grads[pl.ds(mine, count)].astype(F32) + from_core[...].astype(F32)).astype(BF16)
-
-    copies = []
-    for k, device in enumerate(across):
-        rows = pl.ds(pl.multiple_of(device[0] * chunk, chunk), chunk)
-        copies.append(send(half.at[rows], parts.at[k], device, 1 + k))
-    total = half[pl.ds(pl.multiple_of(x * chunk, chunk), chunk)].astype(F32)
-    for k, copy in enumerate(copies):
-        copy.wait()
-        total = total + parts[k].astype(F32)
-
-    line[chip] = total.astype(BF16)
-    copies = [send(line.at[chip], line.at[chip], d, nx + k) for k, d in enumerate(along)]
-    for copy in copies:
-        copy.wait()
-    total = line[0].astype(F32)
-    for k in range(1, ny // 2):
-        total = total + line[k].astype(F32)
-    final[kept] = total.astype(BF16)
-
-    first = nx + len(along)
-    copies = [send(final.at[kept], final.at[kept], d, first + k) for k, d in enumerate(across)]
-    for copy in copies:
-        copy.wait()
-    part = final.at[pl.ds(mine, count)]
-    send(part, part, partner, first + len(across)).wait()
-
-
-def reduce_grads(grads, nx, ny):
+    def finish(copies):
+        for copy in copies:
+            copy.wait()
+
+    def rows(start, size):
+        return pl.ds(pl.multiple_of(start, size), size)
+
+    flights = [
+        [send(grads.at[rows(others + p * part, part)], from_core.at[rows(p * part, part)], partner)]
+        for p in range(3)
+    ]
+    for p in range(3):
+        finish(flights[p])
+        here = rows(p * part, part)
+        kept = grads[rows(mine + p * part, part)].astype(F32)
+        half[here] = (kept + from_core[here].astype(F32)).astype(BF16)
+        flights[p] = []
+        for k in steps:
+            at, device = peer(axes[p][0], k)
+            piece = half.at[rows(p * part + at * size_1, size_1)]
+            flights[p].append(send(piece, got_1.at[3 * p + k - 1], device))
+    for p in range(3):
+        finish(flights[p])
+        total = half[rows(p * part + spot[axes[p][0]] * size_1, size_1)].astype(F32)
+        for k in steps:
+            total = total + got_1[3 * p + k - 1].astype(F32)
+        sum_1[p] = total
+        flights[p] = []
+        for k in steps:
+            at, device = peer(axes[p][1], k)
+            piece = sum_1.at[p, rows(at * size_2, size_2)]
+            flights[p].append(send(piece, got_2.at[3 * p + k - 1], device))
+    for p in range(3):
+        finish(flights[p])
+        total = sum_1[p, rows(spot[axes[p][1]] * size_2, size_2)]
+        for k in steps:
+            total = total + got_2[3 * p + k - 1]
+        sum_2[p] = total
+        flights[p] = []
+        for k in steps:
+            at, device = peer(axes[p][2], k)
+            piece = sum_2.at[p, rows(at * size_3, size_3)]
+            flights[p].append(send(piece, got_3.at[3 * p + k - 1], device))
+    starts = []
+    for p in range(3):
+        start = mine + p * part + spot[axes[p][0]] * size_1
+        middle = start + spot[axes[p][1]] * size_2
+        starts.append((start, middle, middle + spot[axes[p][2]] * size_3))
+
+    def spread(p, level, size):
+        piece = final.at[rows(starts[p][level], size)]
+        return [send(piece, piece, peer(axes[p][level], k)[1]) for k in steps]
+
+    for p in range(3):
+        finish(flights[p])
+        total = sum_2[p, rows(spot[axes[p][2]] * size_3, size_3)]
+        for k in steps:
+            total = total + got_3[3 * p + k - 1]
+        final[rows(starts[p][2], size_3)] = total.astype(BF16)
+        flights[p] = spread(p, 2, size_3)
+    for p in range(3):
+        finish(flights[p])
+        flights[p] = spread(p, 1, size_2)
+    for p in range(3):
+        finish(flights[p])
+        flights[p] = spread(p, 0, size_1)
+    for p in range(3):
+        finish(flights[p])
+        piece = final.at[rows(mine + p * part, part)]
+        flights[p] = [send(piece, piece, partner)]
+    for p in range(3):
+        finish(flights[p])
+
+
+def reduce_grads(grads):
     count = grads.shape[0] // 2
-    sems = 2 * nx + ny // 2 - 1
+    part = count // 3
     return pl.pallas_call(
         reduce_kernel,
         out_shape=jax.ShapeDtypeStruct(grads.shape, BF16),
@@ -439,10 +518,13 @@
         scratch_shapes=[
             pltpu.VMEM((count, C), BF16),
             pltpu.VMEM((count, C), BF16),
-            pltpu.VMEM((nx - 1, count // nx, C), BF16),
-            pltpu.VMEM((ny // 2, count // nx, C), BF16),
-            pltpu.SemaphoreType.DMA((sems,)),
-            pltpu.SemaphoreType.DMA((sems,)),
+            pltpu.VMEM((9, part // 4, C), BF16),
+            pltpu.VMEM((3, part // 4, C), F32),
+            pltpu.VMEM((9, part // 16, C), F32),
+            pltpu.VMEM((3, part // 16, C), F32),
+            pltpu.VMEM((9, part // 64, C), F32),
+            pltpu.SemaphoreType.DMA((60,)),
+            pltpu.SemaphoreType.DMA((60,)),
         ],
         compiler_params=pltpu.CompilerParams(
             collective_id=3, has_side_effects=True, vmem_limit_bytes=LIMIT
@@ -482,33 +564,27 @@
     bias_two,
     cotangent,
 ):
-    x, y = lax.axis_index("gx"), lax.axis_index("gy")
-    nx, ny = lax.axis_size("gx"), lax.axis_size("gy")
     c_in = weight_one.shape[1]
-    lanes = jnp.arange(16, dtype=jnp.int32)
-    table = send_counts[0]
-    outgoing = table[x]
-    incoming = table[:, x]
-    start = jnp.cumsum(outgoing) - outgoing
-    rank = jnp.cumsum(incoming) - incoming
-    hits = (start[None, :] == lanes[:, None]) & (outgoing[None, :] > 0)
-    worker = jnp.sum(jnp.where(hits, lanes[None, :], 0), axis=1)
-    edges = jnp.stack([x > 0, x < nx - 1, y > 0, y < ny - 1]).astype(jnp.int32)
-    info = jnp.concatenate([occupancy.reshape(32), edges, worker.astype(jnp.int32)])
-
-    cots = lax.all_to_all(
-        cotangent[0, 0][jnp.minimum(rank, 7)], "gx", split_axis=0, concat_axis=0, tiled=True
-    )
     mask = voxel_mask[0, 0].reshape(16, 64, 8).astype(F32)
-    *vol_in, order = pl.pallas_call(
+    *vol_in, cots, info, order, sender = pl.pallas_call(
         volume_kernel,
-        out_shape=(VOLUME, FACES, CORNERS, jax.ShapeDtypeStruct((33,), jnp.int32)),
-        in_specs=[SMEM, VMEM, VMEM],
-        out_specs=(VMEM, VMEM, VMEM, SMEM),
+        out_shape=(
+            VOLUME,
+            FACES,
+            CORNERS,
+            jax.ShapeDtypeStruct((16, 8, 8, BRICK), BF16),
+            jax.ShapeDtypeStruct((53,), jnp.int32),
+            jax.ShapeDtypeStruct((33,), jnp.int32),
+            jax.ShapeDtypeStruct((9,), jnp.int32),
+        ),
+        in_specs=[SMEM, SMEM, VMEM, VMEM, VMEM],
+        out_specs=(VMEM,) * 4 + (SMEM,) * 3,
         compiler_params=PARAMS,
         name="volume",
-    )(info, features[0, 0], mask)
+    )(occupancy, send_counts, features[0, 0], mask, cotangent[0, 0])
     halo_in = halo_exchange(*vol_in, 0)
+    halo_in, cots = lax.optimization_barrier((halo_in, cots))
+    cots = lax.all_to_all(cots, "gx", split_axis=0, concat_axis=0, tiled=True)
 
     *hidden, gates = pl.pallas_call(
         first_kernel,
@@ -517,6 +593,7 @@
         out_specs=(VMEM,) * 4,
         scratch_shapes=[WIDE_SCRATCH, BAND_SCRATCH, EVEN_SCRATCH, ODD_SCRATCH, SEMS],
         compiler_params=PARAMS,
+        cost_estimate=pl.CostEstimate(flops=11 * 10**9, bytes_accessed=10**8, transcendentals=0),
         name="first",
     )(info, order, vol_in[0], *halo_in, mask, weight_one, jnp.tile(bias_one, 2)[None])
     halo_mid = halo_exchange(*hidden, 1)
@@ -543,11 +620,9 @@
     halo_back, results = lax.optimization_barrier((halo_back, results))
     arrived = lax.all_to_all(results, "gx", split_axis=0, concat_axis=0, tiled=True)
 
-    mirrored = weight_two[::-1].transpose(0, 2, 1)
-    blocks = (27 * (c_in + C) // 16 + nx * ny - 1) // (nx * ny)
     grads = pl.pallas_call(
         lambda *refs: third_kernel(*refs[:13], c_in, *refs[13:]),
-        out_shape=jax.ShapeDtypeStruct((16 * nx * ny * blocks, C), BF16),
+        out_shape=jax.ShapeDtypeStruct((6144, C), BF16),
         in_specs=[SMEM, SMEM, ANY, ANY, VMEM, VMEM, ANY, ANY, VMEM, VMEM, VMEM, VMEM, VMEM],
         out_specs=VMEM,
         scratch_shapes=[
@@ -557,12 +632,9 @@
         compiler_params=PARAMS,
         cost_estimate=pl.CostEstimate(flops=33 * 10**9, bytes_accessed=10**8, transcendentals=0),
         name="third",
-    )(info, order, slopes[0], *halo_back, vol_in[0], *halo_in, gates, mirrored, grad_two)
-    grads = reduce_grads(grads, nx, ny)
-
-    wanted = jnp.arange(8, dtype=jnp.int32)
-    from_whom = (rank[None, :] == wanted[:, None]) & (incoming[None, :] > 0)
-    sender = jnp.sum(jnp.where(from_whom, lanes[None, :], 0), axis=1)
+    )(info, order, slopes[0], *halo_back, vol_in[0], *halo_in, gates, weight_two, grad_two)
+    grads = reduce_grads(grads)
+
     result, grad_one, grad_two = pl.pallas_call(
         finish_kernel,
         out_shape=(

time: 219 us -> 202 us (0.922)
  local copies, waits for them, and re-layouts: 13 us -> 4.58 us
  Pallas kernels: 189 us -> 184 us
  other arithmetic: 3.16 us -> 0.76 us
    pallas_call x3, Pallas kernels: 62.1 us -> 66 us  [halo_exchange(): pl.pallas_call(halo_kernel, out_shape=(jax.ShapeDtypeStruct((2, 2, 8, LIN...]
    pallas_call x1, Pallas kernels: 24.9 us -> 21.7 us  [body(): pl.pallas_call(second_kernel, out_shape=(VOLUME, FACES, CORNERS, jax.Shap...]
    pallas_call x1, Pallas kernels: 23.8 us -> 21.1 us  [body(): pl.pallas_call(lambda *refs: third_kernel(*refs[:13], c_in, *refs[13:]),...]
    pallas_call x1, Pallas kernels: 51 us -> 48.4 us  [reduce_grads(): pl.pallas_call(reduce_kernel, out_shape=jax.ShapeDtypeStruct(grads.shape,...]
    unnamed x15 -> x8, local copies, waits for them, and re-layouts: 4.38 us -> 2.07 us
  transfers between devices with their start and end apart: 2 -> 2, of which waited for: 0 -> 0; matrix products, arithmetic and copies ran while one was open for 5% -> 0% of each run, Pallas kernels for 63% -> 53%
where the time goes in v3:
time: 202 us
  Pallas kernels  184 us (91%)
  starting transfers between devices  12 us (6%)
  local copies, waits for them, and re-layouts  4.58 us (2%)
    pallas_call x3, Pallas kernels, halo_exchange(): pl.pallas_call(halo_kernel, out_shape=(jax.ShapeDtypeStruct((2, 2, 8, LIN...  66 us
    pallas_call x1, Pallas kernels, reduce_grads(): pl.pallas_call(reduce_kernel, out_shape=jax.ShapeDtypeStruct(grads.shape,...  48.4 us
    pallas_call x1, Pallas kernels, body(): pl.pallas_call(second_kernel, out_shape=(VOLUME, FACES, CORNERS, jax.Shap...  21.7 us
    pallas_call x1, Pallas kernels, body(): pl.pallas_call(lambda *refs: third_kernel(*refs[:13], c_in, *refs[13:]),...  21.1 us
    pallas_call x1, Pallas kernels, body(): pl.pallas_call(first_kernel, out_shape=(VOLUME, FACES, CORNERS, jax.Shape...  13.8 us
    pallas_call x1, Pallas kernels, body(): pl.pallas_call(volume_kernel, out_shape=(VOLUME, FACES, CORNERS, jax.Shap...  8.15 us
    all_to_all x1, starting transfers between devices, body(): cots = lax.all_to_all(cots, 'gx', split_axis=0, concat_axis=0, tiled=True)  6.38 us
    all_to_all x1, starting transfers between devices, body(): lax.all_to_all(results, 'gx', split_axis=0, concat_axis=0, tiled=True)  5.57 us
  transfers between devices with their start and end apart: 2, of which 0 were waited for; matrix products, arithmetic and copies ran while one was open for 0% of the time, Pallas kernels for 53%

profile of v3, /device:TPU:1, one launch (start us, length us, event | category | flops | bytes accessed | tf_op | source)
XLA Modules:
  0.0 201.8 jit_solution(10060646298442633019)
XLA Ops:
  0.6 0.8 convert_element_type.5
  1.4 0.1 copy.12
  1.5 1.2 copy.13.mask
  2.8 8.2 %volume.1 = (bf16[16,2,8,8192]{3,2,1,0:T(8,128)(2,1)}, bf16[2,2,8,8192]{3,2,1,0:T(8,128)(2,1)}, bf16[4,8,1024]{2,1,0:T(8,128)(2,1)}, bf16[16,8,8,1024]{3,2,1,0:T...) custom-call(s32[2,2,8]{2,1,0:T(2,128)} %occupancy.1, s32[1,16,16]{2,1,0:T(8,128)} %counts.1, ...), custom_call_target="tpu_custom_call" | custom-call | tf_op jit(solution)/shard_map/volume/pallas_call | solution.py:569
  10.9 17.3 %halo.3 = (bf16[2,2,8,8192]{3,2,1,0:T(8,128)(2,1)}, bf16[2,2,8,8192]{3,2,1,0:T(8,128)(2,1)}, bf16[4,8,1024]{2,1,0:T(8,128)(2,1)}) custom-call(bf16[16,2,8,8192]{3,2,1,0:T(8,128)(2,1)} %get-tuple-element.42.vol.own.refs_6_, bf16[2,2,8,8192]{3,2,1,0:T(8,128)(2,1)} %get-tuple-element.43.faces, bf16[4,8,1024]{2,1,0:T(8,128)(2,1)} %get-tuple-element.44.corners), custom_call_target="tpu_custom_call" | custom-call | tf_op jit(solution)/shard_map/halo/pallas_call | solution.py:140
  28.2 0.0 copy-start.2
  28.2 6.4 %all-to-all-start = ((bf16[16,8,8,1024]{3,2,1,0:T(8,128)(2,1)}), bf16[16,8,8,1024]{3,2,1,0:T(8,128)(2,1)S(1)}, u32[]{:S(2)}, u32[]{:S(2)}) async-start(bf16[16,8,8,1024]{3,2,1,0:T(8,128)(2,1)} %get-tuple-element.58), calls=%async_computation | async-start | bytes 4194304 | tf_op jit(solution)/shard_map/all_to_all | solution.py:587
  34.6 0.0 copy-done.2
  34.6 0.5 tile.4
  35.2 13.8 %first.1 = (bf16[16,2,8,8192]{3,2,1,0:T(8,128)(2,1)}, bf16[2,2,8,8192]{3,2,1,0:T(8,128)(2,1)}, bf16[4,8,1024]{2,1,0:T(8,128)(2,1)}, bf16[16,256,256]{2,1,0:T(8,128)(2,1)}) custom-call(s32[53]{0:T(128)} %get-tuple-element.40.info.refs_0_, s32[33]{0:T(128)} %get-tuple-element.41.order.refs_1_, bf16[16,2,8,8192]{3,2,1,0:T(8,128)(2,1)} %get-tuple-element.42.vol.own.refs_6_, ...), custom_call_target="tpu_custom_call" | custom-call | flops 11000000512 | bytes 100000000 | tf_op jit(solution)/shard_map/first/pallas_call | solution.py:589
  49.0 0.0 copy-start.3
  49.0 22.8 %halo.4 = (bf16[2,2,8,8192]{3,2,1,0:T(8,128)(2,1)}, bf16[2,2,8,8192]{3,2,1,0:T(8,128)(2,1)}, bf16[4,8,1024]{2,1,0:T(8,128)(2,1)}) custom-call(bf16[16,2,8,8192]{3,2,1,0:T(8,128)(2,1)} %get-tuple-element.52.vol.own, bf16[2,2,8,8192]{3,2,1,0:T(8,128)(2,1)} %get-tuple-element.53.faces, bf16[4,8,1024]{2,1,0:T(8,128)(2,1)} %get-tuple-element.54.corners), custom_call_target="tpu_custom_call" | custom-call | tf_op jit(solution)/shard_map/halo/pallas_call | solution.py:140
  71.8 0.0 all-to-all-done.cots
  71.8 0.0 copy-done.3
  71.9 0.0 copy-start
  71.9 0.6 tile.5
  72.5 0.7 copy-done
  73.2 21.7 %second.1 = (bf16[16,2,8,8192]{3,2,1,0:T(8,128)(2,1)}, bf16[2,2,8,8192]{3,2,1,0:T(8,128)(2,1)}, bf16[4,8,1024]{2,1,0:T(8,128)(2,1)}, bf16[16,8,8,1024]{3,2,1,0:T(8,128)(2,1)}, bf16[3456,128]{1,0:T(8,128)(2,1)}) custom-call(s32[53]{0:T(128)} %get-tuple-element.40.info.refs_0_, s32[33]{0:T(128)} %get-tuple-element.41.order.refs_1_, ...), custom_call_target="tpu_custom_call" | custom-call | tf_op jit(solution)/shard_map/second/pallas_call | solution.py:601
  94.9 25.9 %halo.5 = (bf16[2,2,8,8192]{3,2,1,0:T(8,128)(2,1)}, bf16[2,2,8,8192]{3,2,1,0:T(8,128)(2,1)}, bf16[4,8,1024]{2,1,0:T(8,128)(2,1)}) custom-call(bf16[16,2,8,8192]{3,2,1,0:T(8,128)(2,1)} %get-tuple-element.59.vol.refs_2_, bf16[2,2,8,8192]{3,2,1,0:T(8,128)(2,1)} %get-tuple-element.60.faces, bf16[4,8,1024]{2,1,0:T(8,128)(2,1)} %get-tuple-element.61.corners), custom_call_target="tpu_custom_call" | custom-call | tf_op jit(solution)/shard_map/halo/pallas_call | solution.py:140
  120.8 5.6 %all-to-all-start.1 = ((bf16[16,8,8,1024]{3,2,1,0:T(8,128)(2,1)}), bf16[16,8,8,1024]{3,2,1,0:T(8,128)(2,1)S(1)}, u32[]{:S(2)}, u32[]{:S(2)}) async-start(bf16[16,8,8,1024]{3,2,1,0:T(8,128)(2,1)} %get-tuple-element.71), calls=%async_computation.1 | async-start | bytes 4194304 | tf_op jit(solution)/shard_map/all_to_all | solution.py:621
  126.4 21.1 %third.1.grads = bf16[6144,128]{1,0:T(8,128)(2,1)} custom-call(s32[53]{0:T(128)} %get-tuple-element.40.info.refs_0_, s32[33]{0:T(128)} %get-tuple-element.41.order.refs_1_, bf16[16,2,8,8192]{3,2,1,0:T(8,128)(2,1)} %get-tuple-element.59.vol.refs_2_, bf16[2,2,8,8192]{3,2,1,0:T(8,128)(2,1)} %get-tuple-element.66.refs_3_, ...), custom_call_target="tpu_custom_call" | custom-call | flops 32999999488 | bytes 100000000 | tf_op jit(solution)/shard_map/third/pallas_call | solution.py:623
  147.5 48.4 %reduce.1.grads = bf16[6144,128]{1,0:T(8,128)(2,1)} custom-call(bf16[6144,128]{1,0:T(8,128)(2,1)} %third.1.grads), custom_call_target="tpu_custom_call" | custom-call | tf_op jit(solution)/shard_map/reduce/pallas_call | solution.py:513
  195.9 0.0 all-to-all-done.1.arrived
  195.9 0.0 copy-start.1
  195.9 1.3 copy-done.1
  197.2 4.6 %finish.1 = (bf16[8,8,8,1024]{3,2,1,0:T(8,128)(2,1)}, f32[2592,128]{1,0:T(8,128)}, f32[3456,128]{1,0:T(8,128)}) custom-call(s32[9]{0:T(128)} %get-tuple-element.39.sender, bf16[6144,128]{1,0:T(8,128)(2,1)} %reduce.1.grads, bf16[16,8,8,1024]{3,2,1,0:T(8,128)(2,1)} %copy-done.1), custom_call_target="tpu_custom_call" | custom-call | tf_op jit(solution)/shard_map/finish/pallas_call | solution.py:638
Async XLA Ops:
  28.2 6.4 %copy-start.2 = (f32[128]{0:T(128)S(1)}, f32[128]{0:T(128)}, u32[]{:S(2)}) copy-start(f32[128]{0:T(128)} %param.14) | copy-start | bytes 1540
  28.2 43.6 %all-to-all-start = ((bf16[16,8,8,1024]{3,2,1,0:T(8,128)(2,1)}), bf16[16,8,8,1024]{3,2,1,0:T(8,128)(2,1)S(1)}, u32[]{:S(2)}, u32[]{:S(2)}) async-start(bf16[16,8,8,1024]{3,2,1,0:T(8,128)(2,1)} %get-tuple-element.58), calls=%async_computation | async-start | bytes 4194304 | tf_op jit(solution)/shard_map/all_to_all | solution.py:587
  49.0 22.8 %copy-start.3 = (f32[128]{0:T(128)S(1)}, f32[128]{0:T(128)}, u32[]{:S(2)}) copy-start(f32[128]{0:T(128)} %param.16) | copy-start | bytes 1540
  71.9 1.3 copy-start
  120.8 75.1 %all-to-all-start.1 = ((bf16[16,8,8,1024]{3,2,1,0:T(8,128)(2,1)}), bf16[16,8,8,1024]{3,2,1,0:T(8,128)(2,1)S(1)}, u32[]{:S(2)}, u32[]{:S(2)}) async-start(bf16[16,8,8,1024]{3,2,1,0:T(8,128)(2,1)} %get-tuple-element.71), calls=%async_computation.1 | async-start | bytes 4194304 | tf_op jit(solution)/shard_map/all_to_all | solution.py:621
  195.9 1.3 copy-start.1

commit v4 on v3

v4 whole, which is shorter than its diff:
```python
import functools

import jax
import jax.numpy as jnp
from jax import lax
from jax.experimental import pallas as pl
from jax.experimental.pallas import tpu as pltpu
from jax.sharding import PartitionSpec as P

MESH = pl.DeviceIdType.MESH
F32 = jnp.float32
BF16 = jnp.bfloat16
GROUP = 2
C = 128
BRICK = 8 * C
LINE = 8 * BRICK
WIDE = LINE + 2 * C
PATCH = BRICK + 2 * C
LIMIT = 60 * 1024 * 1024

VMEM = pl.BlockSpec(memory_space=pltpu.VMEM)
SMEM = pl.BlockSpec(memory_space=pltpu.SMEM)
ANY = pl.BlockSpec(memory_space=pl.ANY)

VOLUME = jax.ShapeDtypeStruct((16, 2, 8, LINE), BF16)
FACES = jax.ShapeDtypeStruct((2, 2, 8, LINE), BF16)
CORNERS = jax.ShapeDtypeStruct((4, 8, BRICK), BF16)


def coords(place):
    return lax.div(place, 16), lax.rem(lax.div(place, 8), 2), lax.rem(place, 8)


def put(vol, faces, spot, lane, value):
    xb, yb, zb = spot
    lanes = pl.ds(pl.multiple_of(zb * BRICK + lane, C), value.shape[2])
    vol[pl.ds(xb * 8, 8), yb, :, lanes] = value.astype(BF16)
    row = jnp.where(yb == 0, value[:, 0, :], value[:, 7, :])
    faces[yb, xb, :, lanes] = row.astype(BF16)


def put_corners(faces, corners):
    for side_y in range(2):
        for side_x in range(2):
            face = faces[side_y, side_x].astype(F32)
            row = face[7 * side_x : 7 * side_x + 1]
            rows = [row[:, z * BRICK : (z + 1) * BRICK] for z in range(8)]
            corners[2 * side_y + side_x] = jnp.concatenate(rows, axis=0).astype(BF16)


def volume_kernel(
    occupancy, counts, feat, mask, cotangent,
    vol, faces, corners, cots, info, order, sender,
):
    x = lax.axis_index("gx")

    def sort(place, numbers):
        active, empty = numbers
        xb, yb, zb = coords(place)
        slot = occupancy[xb, yb, zb]
        info[place] = slot
        live = slot >= 0
        order[jnp.where(live, active, 31 - empty)] = place
        one = live.astype(jnp.int32)
        return active + one, empty + 1 - one

    order[32] = lax.fori_loop(0, 32, sort, (0, 0))[0]

    def route(peer, numbers):
        slot, brick = numbers
        info[32 + slot] = peer
        sender[brick] = peer
        cots[peer] = cotangent[jnp.minimum(brick, 7)]
        return slot + counts[0, x, peer], brick + counts[0, peer, x]

    lax.fori_loop(0, 16, route, (0, 0))
    vol[...] = jnp.zeros(vol.shape, BF16)
    faces[...] = jnp.zeros(faces.shape, BF16)
    c_in = feat.shape[3] // 8

    def step(place, _):
        slot = info[place]

        @pl.when(slot >= 0)
        def _():
            rows = feat[slot].astype(F32)
            keep = mask[slot].reshape(8, 8, 8)
            pieces = []
            for w in range(8):
                pieces.append(rows[:, :, w * c_in : (w + 1) * c_in] * keep[:, :, w : w + 1])
                pieces.append(jnp.zeros((8, 8, C - c_in), F32))
            put(vol, faces, coords(place), 0, jnp.concatenate(pieces, axis=2))

        return 0

    lax.fori_loop(0, 32, step, 0)
    put_corners(faces, corners)


def halo_plan(x_faces, faces, corners, x_halo, y_halo, c_halo):
    nx, ny = lax.axis_size("gx"), lax.axis_size("gy")
    x, y = lax.axis_index("gx"), lax.axis_index("gy")
    left, right = lax.rem(x + nx - 1, nx), lax.rem(x + 1, nx)
    down, up = lax.rem(y + ny - 1, ny), lax.rem(y + 1, ny)
    return [
        (x_faces[0], x_halo[1], (left, y)),
        (x_faces[1], x_halo[0], (right, y)),
        (faces.at[0], y_halo.at[1], (x, down)),
        (faces.at[1], y_halo.at[0], (x, up)),
        (corners.at[0], c_halo.at[3], (left, down)),
        (corners.at[1], c_halo.at[2], (right, down)),
        (corners.at[2], c_halo.at[1], (left, up)),
        (corners.at[3], c_halo.at[0], (right, up)),
    ]


def greet(devices):
    barrier = pltpu.get_barrier_semaphore()
    for device in devices:
        pl.semaphore_signal(barrier, inc=1, device_id=device, device_id_type=MESH)
    pl.semaphore_wait(barrier, len(devices))


def sender_of(send_sem, recv_sem):
    used = iter(range(send_sem.shape[0]))

    def send(source, target, device):
        number = next(used)
        copy = pltpu.make_async_remote_copy(
            src_ref=source,
            dst_ref=target,
            send_sem=send_sem.at[number],
            recv_sem=recv_sem.at[number],
            device_id=device,
            device_id_type=MESH,
        )
        copy.start()
        return copy

    return send


def finish(copies):
    for copy in copies:
        copy.wait()


def halo_kernel(vol, faces, corners, x_halo, y_halo, c_halo, send_sem, recv_sem):
    x_faces = (vol.at[0], vol.at[15])
    plan = halo_plan(x_faces, faces, corners, (x_halo.at[0], x_halo.at[1]), y_halo, c_halo)
    greet([device for _, _, device in plan])
    send = sender_of(send_sem, recv_sem)
    finish([send(*item) for item in plan])


def halo_exchange(vol, faces, corners, number):
    return pl.pallas_call(
        halo_kernel,
        out_shape=(jax.ShapeDtypeStruct((2, 2, 8, LINE), BF16), FACES, CORNERS),
        in_specs=[ANY] * 3,
        out_specs=(ANY,) * 3,
        scratch_shapes=[pltpu.SemaphoreType.DMA((8,)), pltpu.SemaphoreType.DMA((8,))],
        compiler_params=pltpu.CompilerParams(collective_id=number, has_side_effects=True),
        name="halo",
    )(vol, faces, corners)


def inside_slab():
    x, y = lax.axis_index("gx"), lax.axis_index("gy")
    nx, ny = lax.axis_size("gx"), lax.axis_size("gy")
    return (x > 0, x < nx - 1), (y > 0, y < ny - 1)


def open_volume(own, x_halo, wide, sems):
    inner = pl.ds(C, LINE)
    copies = [pltpu.make_async_copy(own, wide.at[pl.ds(1, 16), pl.ds(1, 2), :, inner], sems.at[0])]
    if x_halo is not None:
        for end in range(2):
            target = wide.at[17 * end, pl.ds(1, 2), :, inner]
            copies.append(pltpu.make_async_copy(x_halo.at[end], target, sems.at[1 + end]))
    for copy in copies:
        copy.start()
    return copies


def close_volume(y_halo, c_halo, wide, copies):
    inside_x, inside_y = inside_slab()
    inner = pl.ds(C, LINE)
    margin = jnp.zeros((18, 4, 8, C), BF16)
    wide[:, :, :, 0:C] = margin
    wide[:, :, :, C + LINE : WIDE] = margin
    for side in range(2):
        block = 3 * side
        for half in range(2):
            face = jnp.where(inside_y[side], y_halo[side, half].astype(F32), 0.0)
            for row in range(8):
                wide[1 + 8 * half + row, block, :, inner] = jnp.broadcast_to(
                    face[row : row + 1], (8, LINE)
                ).astype(BF16)
        for end in range(2):
            inside = inside_y[side] & inside_x[end]
            corner = jnp.where(inside, c_halo[2 * side + end].astype(F32), 0.0)
            for z in range(8):
                wide[17 * end, block, :, pl.ds(C + z * BRICK, BRICK)] = jnp.broadcast_to(
                    corner[z : z + 1], (8, BRICK)
                ).astype(BF16)
    finish(copies)
    for end in range(2):

        @pl.when(jnp.logical_not(inside_x[end]))
        def _():
            wide[17 * end, 1:3, :, inner] = jnp.zeros((2, 8, LINE), BF16)


def cut_patch(wide, spot, even, odd):
    xb, yb, zb = spot
    lanes = pl.ds(zb * BRICK, PATCH)
    rows = pl.ds(xb * 8, 10)
    before = wide[rows, yb, :, lanes].astype(F32)
    here = wide[rows, yb + 1, :, lanes].astype(F32)
    after = wide[rows, yb + 2, :, lanes].astype(F32)
    line = lax.broadcasted_iota(jnp.int32, here.shape, 1)
    shifts = [
        pltpu.roll(jnp.where(line == 7, before, here), 1, 1),
        here,
        pltpu.roll(jnp.where(line == 0, after, here), 7, 1),
    ]
    for b in range(3):
        even[b] = shifts[b].reshape(80, PATCH).astype(BF16)
        odd[b] = shifts[b][1:9].reshape(64, PATCH).astype(BF16)


def window(even, odd, a, b):
    parts = []
    for g in range(GROUP):
        for j in range(4):
            lanes = pl.ds(2 * C * j, 4 * C)
            parts.append(odd[g, b, :, lanes] if a == 1 else even[g, b, pl.ds(8 * a, 64), lanes])
    return jnp.concatenate(parts, axis=0)


def fill_band(band, taps, mirrored=False):
    depth = taps.shape[1]
    band[...] = jnp.zeros(band.shape, BF16)
    for tap in range(9):
        for c in range(3):
            block = taps[26 - 3 * tap - c].T if mirrored else taps[3 * tap + c]
            for o in range(2):
                band[tap, pl.ds((c + o) * C, depth), pl.ds(o * C, C)] = block


def convolve(even, odd, band):
    total = jnp.zeros((GROUP * 256, 2 * C), F32)
    for a in range(3):
        for b in range(3):
            total = total + jnp.dot(
                window(even, odd, a, b), band[3 * a + b], preferred_element_type=F32
            )
    return total


def add_taps(sums, slopes, even, odd):
    turned = slopes.astype(F32).T.astype(BF16)
    for a in range(3):
        for b in range(3):
            sums[3 * a + b] += jnp.dot(
                turned, window(even, odd, a, b), preferred_element_type=F32
            )


def gather_taps(sums, grad, depth, first):
    for tap in range(9):
        for c in range(3):
            part = (
                sums[tap, 0:C, c * C : (c + 1) * C]
                + sums[tap, C : 2 * C, (c + 1) * C : (c + 2) * C]
            )
            grad[pl.ds(first + (3 * tap + c) * depth, depth)] = part.T[0:depth].astype(BF16)


def groups(info, order, act, start, stop):
    def step(number, _):
        members = []
        for g in range(GROUP):
            position = number * GROUP + g
            place = order[position]
            slot = info[place]
            members.append((position, place, jnp.maximum(slot, 0), slot >= 0))
        act(number, members)
        return 0

    lax.fori_loop(start, stop, step, 0)


def all_groups(info, order, act):
    groups(info, order, act, 0, (order[32] + GROUP - 1) // GROUP)


def spread_mask(keep):
    blocks = []
    for j in range(4):
        pair = [jnp.broadcast_to(keep[:, 2 * j + o : 2 * j + o + 1], (64, C)) for o in range(2)]
        blocks.append(jnp.concatenate(pair, axis=1))
    return jnp.concatenate(blocks, axis=0)


def sigmoid(value):
    return 1.0 / (1.0 + jnp.exp(-value))


def first_kernel(
    info, order, own, x_halo, y_halo, c_halo, mask, taps, bias,
    vol, faces, corners, gates,
    wide, band, even, odd, sems,
):
    copies = open_volume(own, x_halo, wide, sems)
    fill_band(band, taps)
    vol[...] = jnp.zeros(vol.shape, BF16)
    faces[...] = jnp.zeros(faces.shape, BF16)

    def forward(number, members):
        for g, (_, place, _, _) in enumerate(members):
            cut_patch(wide, coords(place), even.at[g], odd.at[g])
        both = convolve(even, odd, band) + bias[...]
        for g, (position, place, slot, live) in enumerate(members):
            linear = both[256 * g : 256 * g + 256]
            keep = jnp.where(live, spread_mask(mask[slot]), 0.0)
            sig = sigmoid(linear)
            hidden = keep * (linear * sig)
            gates[position] = (keep * (sig * (1.0 + linear * (1.0 - sig)))).astype(BF16)
            for j in range(4):
                piece = hidden[64 * j : 64 * j + 64].reshape(8, 8, 2 * C)
                put(vol, faces, coords(place), 2 * C * j, piece)

    close_volume(y_halo, c_halo, wide, copies)
    all_groups(info, order, forward)
    put_corners(faces, corners)


def second_kernel(
    info, order, own, x_halo, y_halo, c_halo, mask, taps, bias, cots,
    vol, faces, corners, results, slopes,
    wide, band, even, odd, sems,
):
    copies = open_volume(own, x_halo, wide, sems)
    fill_band(band, taps)
    vol[...] = jnp.zeros(vol.shape, BF16)
    faces[...] = jnp.zeros(faces.shape, BF16)
    slopes[...] = jnp.zeros(slopes.shape, BF16)

    def forward(number, members):
        for g, (_, place, _, _) in enumerate(members):
            cut_patch(wide, coords(place), even.at[g], odd.at[g])
        both = convolve(even, odd, band) + bias[...]
        for g, (position, place, slot, live) in enumerate(members):
            worker = info[32 + slot]
            linear = both[256 * g : 256 * g + 256]
            keep = jnp.where(live, spread_mask(mask[slot]), 0.0)
            sig = sigmoid(linear)
            output = keep * (linear * sig)
            slope = keep * (sig * (1.0 + linear * (1.0 - sig)))
            for j in range(4):
                rows = slice(64 * j, 64 * j + 64)
                lanes = pl.ds(2 * C * j, 2 * C)
                piece = cots[worker, :, :, lanes].astype(F32).reshape(64, 2 * C) * slope[rows]
                slopes[position, pl.ds(64 * j, 64)] = piece.astype(BF16)
                put(vol, faces, coords(place), 2 * C * j, piece.reshape(8, 8, 2 * C))

            @pl.when(live)
            def _():
                for j in range(4):
                    rows = output[64 * j : 64 * j + 64].reshape(8, 8, 2 * C)
                    results[worker, :, :, pl.ds(2 * C * j, 2 * C)] = rows.astype(BF16)

    close_volume(y_halo, c_halo, wide, copies)
    all_groups(info, order, forward)
    put_corners(faces, corners)


def total_of(grads, final, base, parts, send, buffers):
    x, y = lax.axis_index("gx"), lax.axis_index("gy")
    core = lax.rem(y, 2)
    spot = {"x": x // 4, "z": lax.rem(x, 4), "y": y // 2}
    partner = (x, y + 1 - 2 * core)
    steps = range(1, 4)
    from_core, half, *part_buffers = buffers
    count = half.shape[0]
    mine, others = base + core * count, base + (1 - core) * count

    def peer(axis, k):
        at = lax.rem(spot[axis] + k, 4)
        if axis == "x":
            return at, (4 * at + spot["z"], y)
        if axis == "z":
            return at, (4 * spot["x"] + at, y)
        return at, (x, 2 * at + core)

    def rows(start, size):
        return pl.ds(pl.multiple_of(start, 16), size)

    flights = []
    for offset, size, _ in parts:
        source = grads.at[rows(others + offset, size)]
        flights.append([send(source, from_core.at[pl.ds(offset, size)], partner)])
    yield
    for p, (offset, size, axes) in enumerate(parts):
        finish(flights[p])
        here = pl.ds(offset, size)
        kept = grads[rows(mine + offset, size)].astype(F32)
        half[here] = (kept + from_core[here].astype(F32)).astype(BF16)
        flights[p] = []
        for k in steps:
            at, device = peer(axes[0], k)
            piece = half.at[rows(offset + at * (size // 4), size // 4)]
            flights[p].append(send(piece, part_buffers[4 * p].at[k - 1], device))
    yield
    for p, (offset, size, axes) in enumerate(parts):
        finish(flights[p])
        got, kept, _, _ = part_buffers[4 * p : 4 * p + 4]
        total = half[rows(offset + spot[axes[0]] * (size // 4), size // 4)].astype(F32)
        for k in steps:
            total = total + got[k - 1].astype(F32)
        kept[...] = total
        flights[p] = []
        for k in steps:
            at, device = peer(axes[1], k)
            piece = kept.at[rows(at * (size // 16), size // 16)]
            flights[p].append(send(piece, part_buffers[4 * p + 2].at[k - 1], device))
    yield
    for p, (offset, size, axes) in enumerate(parts):
        finish(flights[p])
        _, kept, got, line = part_buffers[4 * p : 4 * p + 4]
        total = kept[rows(spot[axes[1]] * (size // 16), size // 16)]
        for k in steps:
            total = total + got[k - 1]
        piece = line.at[spot[axes[2]]]
        piece[...] = total
        flights[p] = [send(piece, piece, peer(axes[2], k)[1]) for k in steps]
    yield
    for p, (offset, size, axes) in enumerate(parts):
        finish(flights[p])
        line = part_buffers[4 * p + 3]
        start = mine + offset + spot[axes[0]] * (size // 4) + spot[axes[1]] * (size // 16)
        here = rows(start, size // 16)
        final[here] = (line[0] + line[1] + line[2] + line[3]).astype(BF16)
        piece = final.at[here]
        flights[p] = [send(piece, piece, peer(axes[1], k)[1]) for k in steps]
    yield
    for p, (offset, size, axes) in enumerate(parts):
        finish(flights[p])
        piece = final.at[rows(mine + offset + spot[axes[0]] * (size // 4), size // 4)]
        flights[p] = [send(piece, piece, peer(axes[0], k)[1]) for k in steps]
    yield
    for p, (offset, size, axes) in enumerate(parts):
        finish(flights[p])
        piece = final.at[rows(mine + offset, size)]
        flights[p] = [send(piece, piece, partner)]
    yield
    for flight in flights:
        finish(flight)
    yield


def total_buffers(parts):
    count = sum(size for _, size, _ in parts)
    buffers = [pltpu.VMEM((count, C), BF16)] * 2
    for _, size, _ in parts:
        buffers.append(pltpu.VMEM((3, size // 4, C), BF16))
        buffers.append(pltpu.VMEM((size // 4, C), F32))
        buffers.append(pltpu.VMEM((3, size // 16, C), F32))
        buffers.append(pltpu.VMEM((4, size // 16, C), F32))
    return buffers


PARTS_ONE = ((0, 512, "xzy"), (512, 512, "zyx"), (1024, 512, "yxz"))
PARTS_TWO = ((0, 768, "zxy"), (768, 512, "xyz"), (1280, 512, "yzx"))
ROWS_ONE = 2 * 1536
ROWS_TWO = 2 * 1792


def third_kernel(
    info, order,
    vol, faces, corners, slopes_two,
    own_mid, x_halo_mid, y_halo_mid, c_halo_mid, own_in, x_halo_in, y_halo_in, c_halo_in,
    gates, taps, results, c_in,
    final, arrived,
    grads, wide, wide_other, band, even, odd, sums, slopes, y_halo, c_halo,
    send_sem, recv_sem, sems, sems_other, *buffers,
):
    x, y = lax.axis_index("gx"), lax.axis_index("gy")
    core, chip = lax.rem(y, 2), y // 2
    inner = pl.ds(C, LINE)
    x_halo = [wide.at[17 * end, pl.ds(1, 2), :, inner] for end in range(2)]
    plan = halo_plan((vol.at[0], vol.at[15]), faces, corners, x_halo, y_halo, c_halo)
    devices = [device for _, _, device in plan] + [(x, y + 1 - 2 * core)]
    for k in range(1, 4):
        devices.append((4 * lax.rem(x // 4 + k, 4) + lax.rem(x, 4), y))
        devices.append((4 * (x // 4) + lax.rem(x + k, 4), y))
        devices.append((x, 2 * lax.rem(chip + k, 4) + core))
    workers = [lax.rem(x + k, 16) for k in range(1, 16)]
    devices += [(worker, y) for worker in workers]
    loads_mid = open_volume(own_mid, x_halo_mid, wide_other, sems_other)
    loads = open_volume(vol, None, wide, sems)
    moves = [pltpu.make_async_copy(results.at[x], arrived.at[x], sems.at[1])]
    moves[0].start()
    greet(devices)
    send = sender_of(send_sem, recv_sem)
    halo = [send(*item) for item in plan]
    for worker in workers:
        moves.append(send(results.at[worker], arrived.at[x], (worker, y)))
    buffers_one, buffers_two = buffers[: len(buffers) // 2], buffers[len(buffers) // 2 :]
    total_one = total_of(grads, final, 0, PARTS_ONE, send, buffers_one)
    total_two = total_of(grads, final, ROWS_ONE, PARTS_TWO, send, buffers_two)
    half = 16 // GROUP // 2

    def tap_sums(source):
        def act(number, members):
            for g, (_, place, _, _) in enumerate(members):
                cut_patch(wide_other, coords(place), even.at[g], odd.at[g])
            rows = source[pl.ds(number * GROUP, GROUP)].reshape(GROUP * 256, 2 * C)
            add_taps(sums, rows, even, odd)

        return act

    def back(number, members):
        for g, (_, place, _, _) in enumerate(members):
            cut_patch(wide, coords(place), even.at[g], odd.at[g])
        both = convolve(even, odd, band)
        for g, (position, _, _, live) in enumerate(members):
            rows = both[256 * g : 256 * g + 256] * gates[position].astype(F32)
            slopes[position] = jnp.where(live, rows, 0.0).astype(BF16)

    def clear(first, last):
        grads[first:last] = jnp.zeros((last - first, C), BF16)

    fill_band(band, taps, mirrored=True)
    sums[...] = jnp.zeros(sums.shape, F32)
    clear(27 * c_in, ROWS_ONE)
    clear(ROWS_ONE + 27 * C, ROWS_ONE + ROWS_TWO)
    close_volume(y_halo_mid, c_halo_mid, wide_other, loads_mid)
    groups(info, order, tap_sums(slopes_two), 0, 2 * half)
    gather_taps(sums, grads, C, ROWS_ONE)
    next(total_two)

    loads_in = open_volume(own_in, x_halo_in, wide_other, sems_other)
    sums[...] = jnp.zeros(sums.shape, F32)
    finish(halo)
    close_volume(y_halo, c_halo, wide, loads)
    groups(info, order, back, 0, half)
    next(total_two)
    groups(info, order, back, half, 2 * half)
    next(total_two)
    close_volume(y_halo_in, c_halo_in, wide_other, loads_in)
    groups(info, order, tap_sums(slopes), 0, half)
    next(total_two)
    groups(info, order, tap_sums(slopes), half, 2 * half)
    next(total_two)
    gather_taps(sums, grads, c_in, 0)
    next(total_one)
    for _ in range(3):
        next(total_two)
        next(total_one)
    for _ in range(4):
        next(total_one)
    finish(moves)


def finish_kernel(sender, grads, arrived, result, grad_one, grad_two):
    for number in range(result.shape[0]):
        result[number] = arrived[sender[number]]
    first = 0
    for out in (grad_one, grad_two):
        rows = grads[first : first + out.shape[0]].astype(F32)
        out[...] = rows * lax.rsqrt(jnp.mean(rows * rows) + 1e-05)
        first += ROWS_ONE


WIDE_SCRATCH = pltpu.VMEM((18, 4, 8, WIDE), BF16)
BAND_SCRATCH = pltpu.VMEM((9, 4 * C, 2 * C), BF16)
EVEN_SCRATCH = pltpu.VMEM((GROUP, 3, 80, PATCH), BF16)
ODD_SCRATCH = pltpu.VMEM((GROUP, 3, 64, PATCH), BF16)
SLOPES_SCRATCH = pltpu.VMEM((16, 256, 2 * C), BF16)
SUMS_SCRATCH = pltpu.VMEM((9, 2 * C, 4 * C), F32)
SEMS = pltpu.SemaphoreType.DMA((3,))
PARAMS = pltpu.CompilerParams(vmem_limit_bytes=LIMIT)


def body(
    features,
    voxel_mask,
    occupancy,
    send_counts,
    weight_one,
    bias_one,
    weight_two,
    bias_two,
    cotangent,
):
    c_in = weight_one.shape[1]
    mask = voxel_mask[0, 0].reshape(16, 64, 8).astype(F32)
    *vol_in, cots, info, order, sender = pl.pallas_call(
        volume_kernel,
        out_shape=(
            VOLUME,
            FACES,
            CORNERS,
            jax.ShapeDtypeStruct((16, 8, 8, BRICK), BF16),
            jax.ShapeDtypeStruct((49,), jnp.int32),
            jax.ShapeDtypeStruct((33,), jnp.int32),
            jax.ShapeDtypeStruct((9,), jnp.int32),
        ),
        in_specs=[SMEM, SMEM, VMEM, VMEM, VMEM],
        out_specs=(VMEM,) * 4 + (SMEM,) * 3,
        compiler_params=PARAMS,
        name="volume",
    )(occupancy, send_counts, features[0, 0], mask, cotangent[0, 0])
    halo_in = halo_exchange(*vol_in, 0)
    halo_in, cots = lax.optimization_barrier((halo_in, cots))
    cots = lax.all_to_all(cots, "gx", split_axis=0, concat_axis=0, tiled=True)

    *hidden, gates = pl.pallas_call(
        first_kernel,
        out_shape=(VOLUME, FACES, CORNERS, jax.ShapeDtypeStruct((16, 256, 2 * C), BF16)),
        in_specs=[SMEM, SMEM, ANY, ANY, VMEM, VMEM, VMEM, VMEM, VMEM],
        out_specs=(VMEM,) * 4,
        scratch_shapes=[WIDE_SCRATCH, BAND_SCRATCH, EVEN_SCRATCH, ODD_SCRATCH, SEMS],
        compiler_params=PARAMS,
        cost_estimate=pl.CostEstimate(flops=11 * 10**9, bytes_accessed=10**8, transcendentals=0),
        name="first",
    )(info, order, vol_in[0], *halo_in, mask, weight_one, jnp.tile(bias_one, 2)[None])
    halo_mid = halo_exchange(*hidden, 1)

    *edge, results, slopes = pl.pallas_call(
        second_kernel,
        out_shape=(
            VOLUME,
            FACES,
            CORNERS,
            jax.ShapeDtypeStruct((16, 8, 8, BRICK), BF16),
            jax.ShapeDtypeStruct((16, 256, 2 * C), BF16),
        ),
        in_specs=[SMEM, SMEM, ANY, ANY, VMEM, VMEM, VMEM, VMEM, VMEM, VMEM],
        out_specs=(VMEM,) * 5,
        scratch_shapes=[WIDE_SCRATCH, BAND_SCRATCH, EVEN_SCRATCH, ODD_SCRATCH, SEMS],
        compiler_params=PARAMS,
        name="second",
    )(info, order, hidden[0], *halo_mid, mask, weight_two, jnp.tile(bias_two, 2)[None], cots)
    grads, arrived = pl.pallas_call(
        lambda *refs: third_kernel(*refs[:17], c_in, *refs[17:]),
        out_shape=(
            jax.ShapeDtypeStruct((ROWS_ONE + ROWS_TWO, C), BF16),
            jax.ShapeDtypeStruct((16, 8, 8, BRICK), BF16),
        ),
        in_specs=[SMEM, SMEM, ANY, ANY, ANY, VMEM]
        + [ANY, ANY, VMEM, VMEM, ANY, ANY, VMEM, VMEM]
        + [VMEM, VMEM, ANY],
        out_specs=(VMEM, ANY),
        scratch_shapes=[
            pltpu.VMEM((ROWS_ONE + ROWS_TWO, C), BF16),
            WIDE_SCRATCH, WIDE_SCRATCH, BAND_SCRATCH, EVEN_SCRATCH, ODD_SCRATCH, SUMS_SCRATCH,
            SLOPES_SCRATCH, pltpu.VMEM(FACES.shape, BF16), pltpu.VMEM(CORNERS.shape, BF16),
            pltpu.SemaphoreType.DMA((128,)), pltpu.SemaphoreType.DMA((128,)), SEMS, SEMS,
            *total_buffers(PARTS_ONE), *total_buffers(PARTS_TWO),
        ],
        compiler_params=pltpu.CompilerParams(
            collective_id=3, has_side_effects=True, vmem_limit_bytes=LIMIT
        ),
        cost_estimate=pl.CostEstimate(flops=33 * 10**9, bytes_accessed=10**8, transcendentals=0),
        name="third",
    )(info, order, *edge, slopes, hidden[0], *halo_mid, vol_in[0], *halo_in, gates, weight_two, results)

    result, grad_one, grad_two = pl.pallas_call(
        finish_kernel,
        out_shape=(
            jax.ShapeDtypeStruct((8, 8, 8, BRICK), BF16),
            jax.ShapeDtypeStruct((27 * c_in, C), F32),
            jax.ShapeDtypeStruct((27 * C, C), F32),
        ),
        in_specs=[SMEM, VMEM, VMEM],
        out_specs=(VMEM,) * 3,
        compiler_params=PARAMS,
        name="finish",
    )(sender, grads, arrived)
    return (
        result[None, None],
        grad_one.reshape(weight_one.shape),
        grad_two.reshape(weight_two.shape),
    )


def solution(mesh):
    placed = (
        P("gx", "gy", None, None, None, None),
        P("gx", "gy", None, None),
        P("gx", "gy", None),
        P("gy", None, None),
        P(),
        P(),
        P(),
        P(),
        P("gx", "gy", None, None, None, None),
    )
    return jax.shard_map(
        body,
        mesh=mesh,
        in_specs=placed,
        out_specs=(P("gx", "gy", None, None, None, None), P(), P()),
        check_vma=False,
    )
```

time: 202 us -> 194 us (0.960)
  starting transfers between devices: 12 us -> 5.56 us
    pallas_call x2 -> x1, Pallas kernels: 69.5 us -> 106 us  [body(): pl.pallas_call(lambda *refs: third_kernel(*refs[:17], c_in, *refs[17:]),...]
    pallas_call x3 -> x2, Pallas kernels: 66 us -> 44.3 us  [halo_exchange(): pl.pallas_call(halo_kernel, out_shape=(jax.ShapeDtypeStruct((2, 2, 8, LIN...]
    pallas_call x1, Pallas kernels: 21.7 us -> 11.6 us  [body(): pl.pallas_call(second_kernel, out_shape=(VOLUME, FACES, CORNERS, jax.Shap...]
    all_to_all x1 -> x0, starting transfers between devices: 5.57 us -> none  [body(): lax.all_to_all(results, 'gx', split_axis=0, concat_axis=0, tiled=True)]
    pallas_call x1, Pallas kernels: 13.8 us -> 9.95 us  [body(): pl.pallas_call(first_kernel, out_shape=(VOLUME, FACES, CORNERS, jax.Shape...]
  transfers between devices with their start and end apart: 2 -> 1, of which waited for: 0 -> 0; matrix products, arithmetic and copies ran while one was open for 0% -> 0% of each run, Pallas kernels for 53% -> 19%
where the time goes in v4:
time: 194 us
  Pallas kernels  184 us (95%)
  starting transfers between devices  5.56 us (3%)
  local copies, waits for them, and re-layouts  3.27 us (2%)
    pallas_call x1, Pallas kernels, body(): pl.pallas_call(lambda *refs: third_kernel(*refs[:17], c_in, *refs[17:]),...  106 us
    pallas_call x2, Pallas kernels, halo_exchange(): pl.pallas_call(halo_kernel, out_shape=(jax.ShapeDtypeStruct((2, 2, 8, LIN...  44.3 us
    pallas_call x1, Pallas kernels, body(): pl.pallas_call(second_kernel, out_shape=(VOLUME, FACES, CORNERS, jax.Shap...  11.6 us
    pallas_call x1, Pallas kernels, body(): pl.pallas_call(first_kernel, out_shape=(VOLUME, FACES, CORNERS, jax.Shape...  9.95 us
    pallas_call x1, Pallas kernels, body(): pl.pallas_call(volume_kernel, out_shape=(VOLUME, FACES, CORNERS, jax.Shap...  7.11 us
    all_to_all x1, starting transfers between devices, body(): cots = lax.all_to_all(cots, 'gx', split_axis=0, concat_axis=0, tiled=True)  5.56 us
    pallas_call x1, Pallas kernels, body(): pl.pallas_call(finish_kernel, out_shape=(jax.ShapeDtypeStruct((8, 8, 8, B...  4.64 us
  transfers between devices with their start and end apart: 1, of which 0 were waited for; matrix products, arithmetic and copies ran while one was open for 0% of the time, Pallas kernels for 19%

profile of v4, /device:TPU:1, one launch (start us, length us, event | category | flops | bytes accessed | tf_op | source)
XLA Modules:
  0.0 194.0 jit_solution(14874906940679842297)
XLA Ops:
  0.6 0.8 convert_element_type.5
  1.4 0.1 copy.12
  1.5 1.2 copy.13.mask
  2.8 7.1 %volume.1 = (bf16[16,2,8,8192]{3,2,1,0:T(8,128)(2,1)}, bf16[2,2,8,8192]{3,2,1,0:T(8,128)(2,1)}, bf16[4,8,1024]{2,1,0:T(8,128)(2,1)}, bf16[16,8,8,1024]{3,2,1,0:T...) custom-call(s32[2,2,8]{2,1,0:T(2,128)} %occupancy.1, s32[1,16,16]{2,1,0:T(8,128)} %counts.1, ...), custom_call_target="tpu_custom_call" | custom-call | tf_op jit(solution)/shard_map/volume/pallas_call | solution.py:601
  9.9 17.8 %halo.2 = (bf16[2,2,8,8192]{3,2,1,0:T(8,128)(2,1)}, bf16[2,2,8,8192]{3,2,1,0:T(8,128)(2,1)}, bf16[4,8,1024]{2,1,0:T(8,128)(2,1)}) custom-call(bf16[16,2,8,8192]{3,2,1,0:T(8,128)(2,1)} %get-tuple-element.37.vol.own.refs_10_, bf16[2,2,8,8192]{3,2,1,0:T(8,128)(2,1)} %get-tuple-element.38.faces, bf16[4,8,1024]{2,1,0:T(8,128)(2,1)} %get-tuple-element.39.corners), custom_call_target="tpu_custom_call" | custom-call | tf_op jit(solution)/shard_map/halo/pallas_call | solution.py:157
  27.7 0.0 copy-start.1
  27.7 5.6 %all-to-all-start = ((bf16[16,8,8,1024]{3,2,1,0:T(8,128)(2,1)}), bf16[16,8,8,1024]{3,2,1,0:T(8,128)(2,1)S(1)}, u32[]{:S(2)}, u32[]{:S(2)}) async-start(bf16[16,8,8,1024]{3,2,1,0:T(8,128)(2,1)} %get-tuple-element.53), calls=%async_computation | async-start | bytes 4194304 | tf_op jit(solution)/shard_map/all_to_all | solution.py:619
  33.2 0.0 copy-done.1
  33.3 0.6 tile.4
  33.8 9.9 %first.1 = (bf16[16,2,8,8192]{3,2,1,0:T(8,128)(2,1)}, bf16[2,2,8,8192]{3,2,1,0:T(8,128)(2,1)}, bf16[4,8,1024]{2,1,0:T(8,128)(2,1)}, bf16[16,256,256]{2,1,0:T(8,128)(2,1)}) custom-call(s32[49]{0:T(128)} %get-tuple-element.35.info.refs_0_, s32[33]{0:T(128)} %get-tuple-element.36.order.refs_1_, bf16[16,2,8,8192]{3,2,1,0:T(8,128)(2,1)} %get-tuple-element.37.vol.own.refs_10_, ...), custom_call_target="tpu_custom_call" | custom-call | flops 11000000512 | bytes 100000000 | tf_op jit(solution)/shard_map/first/pallas_call | solution.py:621
  43.8 0.0 copy-start.2
  43.8 26.5 %halo.3 = (bf16[2,2,8,8192]{3,2,1,0:T(8,128)(2,1)}, bf16[2,2,8,8192]{3,2,1,0:T(8,128)(2,1)}, bf16[4,8,1024]{2,1,0:T(8,128)(2,1)}) custom-call(bf16[16,2,8,8192]{3,2,1,0:T(8,128)(2,1)} %get-tuple-element.47.vol.own.refs_6_, bf16[2,2,8,8192]{3,2,1,0:T(8,128)(2,1)} %get-tuple-element.48.faces, bf16[4,8,1024]{2,1,0:T(8,128)(2,1)} %get-tuple-element.49.corners), custom_call_target="tpu_custom_call" | custom-call | tf_op jit(solution)/shard_map/halo/pallas_call | solution.py:157
  70.3 0.0 all-to-all-done.cots
  70.3 0.0 copy-done.2
  70.3 0.0 copy-start
  70.3 0.7 tile.5
  71.0 0.7 copy-done
  71.7 11.6 %second.1 = (bf16[16,2,8,8192]{3,2,1,0:T(8,128)(2,1)}, bf16[2,2,8,8192]{3,2,1,0:T(8,128)(2,1)}, bf16[4,8,1024]{2,1,0:T(8,128)(2,1)}, bf16[16,8,8,1024]{3,2,1,0:T(8,128)(2,1)}, bf16[16,256,256]{2,1,0:T(8,128)(2,1)}) custom-call(s32[49]{0:T(128)} %get-tuple-element.35.info.refs_0_, s32[33]{0:T(128)} %get-tuple-element.36.order.refs_1_, ...), custom_call_target="tpu_custom_call" | custom-call | tf_op jit(solution)/shard_map/second/pallas_call | solution.py:633
  83.2 106.1 %third.1 = (bf16[6656,128]{1,0:T(8,128)(2,1)}, bf16[16,8,8,1024]{3,2,1,0:T(8,128)(2,1)}) custom-call(s32[49]{0:T(128)} %get-tuple-element.35.info.refs_0_, s32[33]{0:T(128)} %get-tuple-element.36.order.refs_1_, bf16[16,2,8,8192]{3,2,1,0:T(8,128)(2,1)} %get-tuple-element.54.refs_2_, bf16[2,2,8,8192]{3,2,1,0:T(8,128)(2,1)} %get-tuple-element.55.refs_3_, ...), custom_call_target="tpu_custom_call" | custom-call | flops 32999999488 | bytes 100000000 | tf_op jit(solution)/shard_map/third/pallas_call | solution.py:648
  189.3 4.6 %finish.1 = (bf16[8,8,8,1024]{3,2,1,0:T(8,128)(2,1)}, f32[2592,128]{1,0:T(8,128)}, f32[3456,128]{1,0:T(8,128)}) custom-call(s32[9]{0:T(128)} %get-tuple-element.34.sender, bf16[6656,128]{1,0:T(8,128)(2,1)} %get-tuple-element.60.grads, bf16[16,8,8,1024]{3,2,1,0:T(8,128)(2,1)} %get-tuple-element.61.arrived), custom_call_target="tpu_custom_call" | custom-call | tf_op jit(solution)/shard_map/finish/pallas_call | solution.py:672
Async XLA Ops:
  27.7 5.6 %copy-start.1 = (f32[128]{0:T(128)S(1)}, f32[128]{0:T(128)}, u32[]{:S(2)}) copy-start(f32[128]{0:T(128)} %param.14) | copy-start | bytes 1540
  27.7 42.6 %all-to-all-start = ((bf16[16,8,8,1024]{3,2,1,0:T(8,128)(2,1)}), bf16[16,8,8,1024]{3,2,1,0:T(8,128)(2,1)S(1)}, u32[]{:S(2)}, u32[]{:S(2)}) async-start(bf16[16,8,8,1024]{3,2,1,0:T(8,128)(2,1)} %get-tuple-element.53), calls=%async_computation | async-start | bytes 4194304 | tf_op jit(solution)/shard_map/all_to_all | solution.py:619
  43.8 26.5 %copy-start.2 = (f32[128]{0:T(128)S(1)}, f32[128]{0:T(128)}, u32[]{:S(2)}) copy-start(f32[128]{0:T(128)} %param.16) | copy-start | bytes 1540
  70.3 1.3 copy-start

commit v5 on v4

--- a/solution.py
+++ b/solution.py
@@ -511,7 +511,7 @@
     buffers_one, buffers_two = buffers[: len(buffers) // 2], buffers[len(buffers) // 2 :]
     total_one = total_of(grads, final, 0, PARTS_ONE, send, buffers_one)
     total_two = total_of(grads, final, ROWS_ONE, PARTS_TWO, send, buffers_two)
-    half = 16 // GROUP // 2
+    count = 16 // GROUP
 
     def tap_sums(source):
         def act(number, members):
@@ -538,7 +538,7 @@
     clear(27 * c_in, ROWS_ONE)
     clear(ROWS_ONE + 27 * C, ROWS_ONE + ROWS_TWO)
     close_volume(y_halo_mid, c_halo_mid, wide_other, loads_mid)
-    groups(info, order, tap_sums(slopes_two), 0, 2 * half)
+    groups(info, order, tap_sums(slopes_two), 0, count)
     gather_taps(sums, grads, C, ROWS_ONE)
     next(total_two)
 
@@ -546,22 +546,16 @@
     sums[...] = jnp.zeros(sums.shape, F32)
     finish(halo)
     close_volume(y_halo, c_halo, wide, loads)
-    groups(info, order, back, 0, half)
-    next(total_two)
-    groups(info, order, back, half, 2 * half)
+    groups(info, order, back, 0, count)
     next(total_two)
     close_volume(y_halo_in, c_halo_in, wide_other, loads_in)
-    groups(info, order, tap_sums(slopes), 0, half)
-    next(total_two)
-    groups(info, order, tap_sums(slopes), half, 2 * half)
-    next(total_two)
+    groups(info, order, tap_sums(slopes), 0, count)
     gather_taps(sums, grads, c_in, 0)
+    for _ in range(6):
+        next(total_one)
+        next(total_two)
     next(total_one)
-    for _ in range(3):
-        next(total_two)
-        next(total_one)
-    for _ in range(4):
-        next(total_one)
+    next(total_one)
     finish(moves)
 
 

time: 194 us -> 185 us (0.954)
  Pallas kernels: 184 us -> 175 us
    pallas_call x1, Pallas kernels: 106 us -> 85.6 us  [body(): pl.pallas_call(lambda *refs: third_kernel(*refs[:17], c_in, *refs[17:]),...]
    pallas_call x2, Pallas kernels: 44.3 us -> 33.1 us  [halo_exchange(): pl.pallas_call(halo_kernel, out_shape=(jax.ShapeDtypeStruct((2, 2, 8, LIN...]
    pallas_call x1, Pallas kernels: 11.6 us -> 21.7 us  [body(): pl.pallas_call(second_kernel, out_shape=(VOLUME, FACES, CORNERS, jax.Shap...]
    pallas_call x1, Pallas kernels: 9.95 us -> 19.7 us  [body(): pl.pallas_call(first_kernel, out_shape=(VOLUME, FACES, CORNERS, jax.Shape...]
    pallas_call x1, Pallas kernels: 7.11 us -> 10.1 us  [body(): pl.pallas_call(volume_kernel, out_shape=(VOLUME, FACES, CORNERS, jax.Shap...]
  transfers between devices with their start and end apart: 1 -> 1, of which waited for: 0 -> 0; matrix products, arithmetic and copies ran while one was open for 0% -> 0% of each run, Pallas kernels for 19% -> 20%
where the time goes in v5:
time: 185 us
  Pallas kernels  175 us (95%)
  starting transfers between devices  5.51 us (3%)
  local copies, waits for them, and re-layouts  3.27 us (2%)
    pallas_call x1, Pallas kernels, body(): pl.pallas_call(lambda *refs: third_kernel(*refs[:17], c_in, *refs[17:]),...  85.6 us
    pallas_call x2, Pallas kernels, halo_exchange(): pl.pallas_call(halo_kernel, out_shape=(jax.ShapeDtypeStruct((2, 2, 8, LIN...  33.1 us
    pallas_call x1, Pallas kernels, body(): pl.pallas_call(second_kernel, out_shape=(VOLUME, FACES, CORNERS, jax.Shap...  21.7 us
    pallas_call x1, Pallas kernels, body(): pl.pallas_call(first_kernel, out_shape=(VOLUME, FACES, CORNERS, jax.Shape...  19.7 us
    pallas_call x1, Pallas kernels, body(): pl.pallas_call(volume_kernel, out_shape=(VOLUME, FACES, CORNERS, jax.Shap...  10.1 us
    all_to_all x1, starting transfers between devices, body(): cots = lax.all_to_all(cots, 'gx', split_axis=0, concat_axis=0, tiled=True)  5.51 us
    pallas_call x1, Pallas kernels, body(): pl.pallas_call(finish_kernel, out_shape=(jax.ShapeDtypeStruct((8, 8, 8, B...  4.64 us
  transfers between devices with their start and end apart: 1, of which 0 were waited for; matrix products, arithmetic and copies ran while one was open for 0% of the time, Pallas kernels for 20%

profile of v5, /device:TPU:1, one launch (start us, length us, event | category | flops | bytes accessed | tf_op | source)
XLA Modules:
  0.0 185.2 jit_solution(3613800548656076068)
XLA Ops:
  0.6 0.8 convert_element_type.5
  1.4 0.1 copy.12
  1.5 1.2 copy.13.mask
  2.8 10.1 %volume.1 = (bf16[16,2,8,8192]{3,2,1,0:T(8,128)(2,1)}, bf16[2,2,8,8192]{3,2,1,0:T(8,128)(2,1)}, bf16[4,8,1024]{2,1,0:T(8,128)(2,1)}, bf16[16,8,8,1024]{3,2,1,0:T...) custom-call(s32[2,2,8]{2,1,0:T(2,128)} %occupancy.1, s32[1,16,16]{2,1,0:T(8,128)} %counts.1, ...), custom_call_target="tpu_custom_call" | custom-call | tf_op jit(solution)/shard_map/volume/pallas_call | solution.py:595
  12.9 15.2 %halo.2 = (bf16[2,2,8,8192]{3,2,1,0:T(8,128)(2,1)}, bf16[2,2,8,8192]{3,2,1,0:T(8,128)(2,1)}, bf16[4,8,1024]{2,1,0:T(8,128)(2,1)}) custom-call(bf16[16,2,8,8192]{3,2,1,0:T(8,128)(2,1)} %get-tuple-element.37.vol.own.refs_10_, bf16[2,2,8,8192]{3,2,1,0:T(8,128)(2,1)} %get-tuple-element.38.faces, bf16[4,8,1024]{2,1,0:T(8,128)(2,1)} %get-tuple-element.39.corners), custom_call_target="tpu_custom_call" | custom-call | tf_op jit(solution)/shard_map/halo/pallas_call | solution.py:157
  28.0 0.0 copy-start.1
  28.1 5.5 %all-to-all-start = ((bf16[16,8,8,1024]{3,2,1,0:T(8,128)(2,1)}), bf16[16,8,8,1024]{3,2,1,0:T(8,128)(2,1)S(1)}, u32[]{:S(2)}, u32[]{:S(2)}) async-start(bf16[16,8,8,1024]{3,2,1,0:T(8,128)(2,1)} %get-tuple-element.53), calls=%async_computation | async-start | bytes 4194304 | tf_op jit(solution)/shard_map/all_to_all | solution.py:613
  33.6 0.0 copy-done.1
  33.6 0.6 tile.4
  34.2 19.7 %first.1 = (bf16[16,2,8,8192]{3,2,1,0:T(8,128)(2,1)}, bf16[2,2,8,8192]{3,2,1,0:T(8,128)(2,1)}, bf16[4,8,1024]{2,1,0:T(8,128)(2,1)}, bf16[16,256,256]{2,1,0:T(8,128)(2,1)}) custom-call(s32[49]{0:T(128)} %get-tuple-element.35.info.refs_0_, s32[33]{0:T(128)} %get-tuple-element.36.order.refs_1_, bf16[16,2,8,8192]{3,2,1,0:T(8,128)(2,1)} %get-tuple-element.37.vol.own.refs_10_, ...), custom_call_target="tpu_custom_call" | custom-call | flops 11000000512 | bytes 100000000 | tf_op jit(solution)/shard_map/first/pallas_call | solution.py:615
  53.9 0.0 copy-start.2
  53.9 17.9 %halo.3 = (bf16[2,2,8,8192]{3,2,1,0:T(8,128)(2,1)}, bf16[2,2,8,8192]{3,2,1,0:T(8,128)(2,1)}, bf16[4,8,1024]{2,1,0:T(8,128)(2,1)}) custom-call(bf16[16,2,8,8192]{3,2,1,0:T(8,128)(2,1)} %get-tuple-element.47.vol.own.refs_6_, bf16[2,2,8,8192]{3,2,1,0:T(8,128)(2,1)} %get-tuple-element.48.faces, bf16[4,8,1024]{2,1,0:T(8,128)(2,1)} %get-tuple-element.49.corners), custom_call_target="tpu_custom_call" | custom-call | tf_op jit(solution)/shard_map/halo/pallas_call | solution.py:157
  71.9 0.0 all-to-all-done.cots
  71.9 0.0 copy-done.2
  71.9 0.0 copy-start
  71.9 0.7 tile.5
  72.5 0.7 copy-done
  73.2 21.7 %second.1 = (bf16[16,2,8,8192]{3,2,1,0:T(8,128)(2,1)}, bf16[2,2,8,8192]{3,2,1,0:T(8,128)(2,1)}, bf16[4,8,1024]{2,1,0:T(8,128)(2,1)}, bf16[16,8,8,1024]{3,2,1,0:T(8,128)(2,1)}, bf16[16,256,256]{2,1,0:T(8,128)(2,1)}) custom-call(s32[49]{0:T(128)} %get-tuple-element.35.info.refs_0_, s32[33]{0:T(128)} %get-tuple-element.36.order.refs_1_, ...), custom_call_target="tpu_custom_call" | custom-call | tf_op jit(solution)/shard_map/second/pallas_call | solution.py:627
  94.9 85.6 %third.1 = (bf16[6656,128]{1,0:T(8,128)(2,1)}, bf16[16,8,8,1024]{3,2,1,0:T(8,128)(2,1)}) custom-call(s32[49]{0:T(128)} %get-tuple-element.35.info.refs_0_, s32[33]{0:T(128)} %get-tuple-element.36.order.refs_1_, bf16[16,2,8,8192]{3,2,1,0:T(8,128)(2,1)} %get-tuple-element.54.refs_2_, bf16[2,2,8,8192]{3,2,1,0:T(8,128)(2,1)} %get-tuple-element.55.refs_3_, ...), custom_call_target="tpu_custom_call" | custom-call | flops 32999999488 | bytes 100000000 | tf_op jit(solution)/shard_map/third/pallas_call | solution.py:642
  180.5 4.6 %finish.1 = (bf16[8,8,8,1024]{3,2,1,0:T(8,128)(2,1)}, f32[2592,128]{1,0:T(8,128)}, f32[3456,128]{1,0:T(8,128)}) custom-call(s32[9]{0:T(128)} %get-tuple-element.34.sender, bf16[6656,128]{1,0:T(8,128)(2,1)} %get-tuple-element.60.grads, bf16[16,8,8,1024]{3,2,1,0:T(8,128)(2,1)} %get-tuple-element.61.arrived), custom_call_target="tpu_custom_call" | custom-call | tf_op jit(solution)/shard_map/finish/pallas_call | solution.py:666
Async XLA Ops:
  28.0 5.5 %copy-start.1 = (f32[128]{0:T(128)S(1)}, f32[128]{0:T(128)}, u32[]{:S(2)}) copy-start(f32[128]{0:T(128)} %param.14) | copy-start | bytes 1540
  28.1 43.8 %all-to-all-start = ((bf16[16,8,8,1024]{3,2,1,0:T(8,128)(2,1)}), bf16[16,8,8,1024]{3,2,1,0:T(8,128)(2,1)S(1)}, u32[]{:S(2)}, u32[]{:S(2)}) async-start(bf16[16,8,8,1024]{3,2,1,0:T(8,128)(2,1)} %get-tuple-element.53), calls=%async_computation | async-start | bytes 4194304 | tf_op jit(solution)/shard_map/all_to_all | solution.py:613
  53.9 18.0 %copy-start.2 = (f32[128]{0:T(128)S(1)}, f32[128]{0:T(128)}, u32[]{:S(2)}) copy-start(f32[128]{0:T(128)} %param.16) | copy-start | bytes 1540
  71.9 1.3 copy-start

commit v6 on v5

--- a/solution.py
+++ b/solution.py
@@ -10,7 +10,7 @@
 MESH = pl.DeviceIdType.MESH
 F32 = jnp.float32
 BF16 = jnp.bfloat16
-GROUP = 2
+GROUP = 4
 C = 128
 BRICK = 8 * C
 LINE = 8 * BRICK

time: 185 us -> 182 us (0.984)
  Pallas kernels: 175 us -> 173 us
    pallas_call x1, Pallas kernels: 85.6 us -> 83 us  [body(): pl.pallas_call(lambda *refs: third_kernel(*refs[:17], c_in, *refs[17:]),...]
where the time goes in v6:
time: 182 us; the launch traced here: 183 us
  Pallas kernels  173 us (95%)
  starting transfers between devices  5.87 us (3%)
  local copies, waits for them, and re-layouts  3.27 us (2%)
    pallas_call x1, Pallas kernels, body(): pl.pallas_call(lambda *refs: third_kernel(*refs[:17], c_in, *refs[17:]),...  83 us
    pallas_call x2, Pallas kernels, halo_exchange(): pl.pallas_call(halo_kernel, out_shape=(jax.ShapeDtypeStruct((2, 2, 8, LIN...  33.9 us
    pallas_call x1, Pallas kernels, body(): pl.pallas_call(second_kernel, out_shape=(VOLUME, FACES, CORNERS, jax.Shap...  22 us
    pallas_call x1, Pallas kernels, body(): pl.pallas_call(first_kernel, out_shape=(VOLUME, FACES, CORNERS, jax.Shape...  19.2 us
    pallas_call x1, Pallas kernels, body(): pl.pallas_call(volume_kernel, out_shape=(VOLUME, FACES, CORNERS, jax.Shap...  9.85 us
    all_to_all x1, starting transfers between devices, body(): cots = lax.all_to_all(cots, 'gx', split_axis=0, concat_axis=0, tiled=True)  5.87 us
    pallas_call x1, Pallas kernels, body(): pl.pallas_call(finish_kernel, out_shape=(jax.ShapeDtypeStruct((8, 8, 8, B...  4.64 us
  transfers between devices with their start and end apart: 1, of which 0 were waited for; matrix products, arithmetic and copies ran while one was open for 0% of the time, Pallas kernels for 20%

profile of v6, /device:TPU:1, one launch (start us, length us, event | category | flops | bytes accessed | tf_op | source)
XLA Modules:
  0.0 183.2 jit_solution(15424760034088187395)
XLA Ops:
  0.6 0.8 convert_element_type.5
  1.4 0.1 copy.12
  1.5 1.2 copy.13.mask
  2.8 9.9 %volume.1 = (bf16[16,2,8,8192]{3,2,1,0:T(8,128)(2,1)}, bf16[2,2,8,8192]{3,2,1,0:T(8,128)(2,1)}, bf16[4,8,1024]{2,1,0:T(8,128)(2,1)}, bf16[16,8,8,1024]{3,2,1,0:T...) custom-call(s32[2,2,8]{2,1,0:T(2,128)} %occupancy.1, s32[1,16,16]{2,1,0:T(8,128)} %counts.1, ...), custom_call_target="tpu_custom_call" | custom-call | tf_op jit(solution)/shard_map/volume/pallas_call | solution.py:595
  12.6 16.5 %halo.2 = (bf16[2,2,8,8192]{3,2,1,0:T(8,128)(2,1)}, bf16[2,2,8,8192]{3,2,1,0:T(8,128)(2,1)}, bf16[4,8,1024]{2,1,0:T(8,128)(2,1)}) custom-call(bf16[16,2,8,8192]{3,2,1,0:T(8,128)(2,1)} %get-tuple-element.37.vol.own.refs_10_, bf16[2,2,8,8192]{3,2,1,0:T(8,128)(2,1)} %get-tuple-element.38.faces, bf16[4,8,1024]{2,1,0:T(8,128)(2,1)} %get-tuple-element.39.corners), custom_call_target="tpu_custom_call" | custom-call | tf_op jit(solution)/shard_map/halo/pallas_call | solution.py:157
  29.2 0.0 copy-start.1
  29.2 5.9 %all-to-all-start = ((bf16[16,8,8,1024]{3,2,1,0:T(8,128)(2,1)}), bf16[16,8,8,1024]{3,2,1,0:T(8,128)(2,1)S(1)}, u32[]{:S(2)}, u32[]{:S(2)}) async-start(bf16[16,8,8,1024]{3,2,1,0:T(8,128)(2,1)} %get-tuple-element.53), calls=%async_computation | async-start | bytes 4194304 | tf_op jit(solution)/shard_map/all_to_all | solution.py:613
  35.0 0.0 copy-done.1
  35.1 0.6 tile.4
  35.6 19.2 %first.1 = (bf16[16,2,8,8192]{3,2,1,0:T(8,128)(2,1)}, bf16[2,2,8,8192]{3,2,1,0:T(8,128)(2,1)}, bf16[4,8,1024]{2,1,0:T(8,128)(2,1)}, bf16[16,256,256]{2,1,0:T(8,128)(2,1)}) custom-call(s32[49]{0:T(128)} %get-tuple-element.35.info.refs_0_, s32[33]{0:T(128)} %get-tuple-element.36.order.refs_1_, bf16[16,2,8,8192]{3,2,1,0:T(8,128)(2,1)} %get-tuple-element.37.vol.own.refs_10_, ...), custom_call_target="tpu_custom_call" | custom-call | flops 11000000512 | bytes 100000000 | tf_op jit(solution)/shard_map/first/pallas_call | solution.py:615
  54.8 0.0 copy-start.2
  54.9 17.4 %halo.3 = (bf16[2,2,8,8192]{3,2,1,0:T(8,128)(2,1)}, bf16[2,2,8,8192]{3,2,1,0:T(8,128)(2,1)}, bf16[4,8,1024]{2,1,0:T(8,128)(2,1)}) custom-call(bf16[16,2,8,8192]{3,2,1,0:T(8,128)(2,1)} %get-tuple-element.47.vol.own.refs_6_, bf16[2,2,8,8192]{3,2,1,0:T(8,128)(2,1)} %get-tuple-element.48.faces, bf16[4,8,1024]{2,1,0:T(8,128)(2,1)} %get-tuple-element.49.corners), custom_call_target="tpu_custom_call" | custom-call | tf_op jit(solution)/shard_map/halo/pallas_call | solution.py:157
  72.3 0.0 all-to-all-done.cots
  72.3 0.0 copy-done.2
  72.3 0.0 copy-start
  72.3 0.7 tile.5
  73.0 0.7 copy-done
  73.6 22.0 %second.1 = (bf16[16,2,8,8192]{3,2,1,0:T(8,128)(2,1)}, bf16[2,2,8,8192]{3,2,1,0:T(8,128)(2,1)}, bf16[4,8,1024]{2,1,0:T(8,128)(2,1)}, bf16[16,8,8,1024]{3,2,1,0:T(8,128)(2,1)}, bf16[16,256,256]{2,1,0:T(8,128)(2,1)}) custom-call(s32[49]{0:T(128)} %get-tuple-element.35.info.refs_0_, s32[33]{0:T(128)} %get-tuple-element.36.order.refs_1_, ...), custom_call_target="tpu_custom_call" | custom-call | tf_op jit(solution)/shard_map/second/pallas_call | solution.py:627
  95.6 83.0 %third.1 = (bf16[6656,128]{1,0:T(8,128)(2,1)}, bf16[16,8,8,1024]{3,2,1,0:T(8,128)(2,1)}) custom-call(s32[49]{0:T(128)} %get-tuple-element.35.info.refs_0_, s32[33]{0:T(128)} %get-tuple-element.36.order.refs_1_, bf16[16,2,8,8192]{3,2,1,0:T(8,128)(2,1)} %get-tuple-element.54.refs_2_, bf16[2,2,8,8192]{3,2,1,0:T(8,128)(2,1)} %get-tuple-element.55.refs_3_, ...), custom_call_target="tpu_custom_call" | custom-call | flops 32999999488 | bytes 100000000 | tf_op jit(solution)/shard_map/third/pallas_call | solution.py:642
  178.6 4.6 %finish.1 = (bf16[8,8,8,1024]{3,2,1,0:T(8,128)(2,1)}, f32[2592,128]{1,0:T(8,128)}, f32[3456,128]{1,0:T(8,128)}) custom-call(s32[9]{0:T(128)} %get-tuple-element.34.sender, bf16[6656,128]{1,0:T(8,128)(2,1)} %get-tuple-element.60.grads, bf16[16,8,8,1024]{3,2,1,0:T(8,128)(2,1)} %get-tuple-element.61.arrived), custom_call_target="tpu_custom_call" | custom-call | tf_op jit(solution)/shard_map/finish/pallas_call | solution.py:666
Async XLA Ops:
  29.2 5.9 %copy-start.1 = (f32[128]{0:T(128)S(1)}, f32[128]{0:T(128)}, u32[]{:S(2)}) copy-start(f32[128]{0:T(128)} %param.14) | copy-start | bytes 1540
  29.2 43.1 %all-to-all-start = ((bf16[16,8,8,1024]{3,2,1,0:T(8,128)(2,1)}), bf16[16,8,8,1024]{3,2,1,0:T(8,128)(2,1)S(1)}, u32[]{:S(2)}, u32[]{:S(2)}) async-start(bf16[16,8,8,1024]{3,2,1,0:T(8,128)(2,1)} %get-tuple-element.53), calls=%async_computation | async-start | bytes 4194304 | tf_op jit(solution)/shard_map/all_to_all | solution.py:613
  54.8 17.5 %copy-start.2 = (f32[128]{0:T(128)S(1)}, f32[128]{0:T(128)}, u32[]{:S(2)}) copy-start(f32[128]{0:T(128)} %param.16) | copy-start | bytes 1540
  72.3 1.3 copy-start
